TPU v7x, 256 devices: a whole 4x4x8 slice. The times are simulated.
256 devices in a mesh: row: 16 (over z, x_hi), col: 8 (over y, x_lo), depth: 2 (over core).
Axes of the slice: x: 4 (x_hi: 2, x_lo: 2; x = x_hi * 2 + x_lo), y: 4, z: 8, core: 2. Of those that a mesh axis runs over, the one named last changes fastest.
Arguments:
- amplitudes: float32 [512, 65536], P('row', ('col', 'depth')), may hold values from -6 to 6
- integrals: float32 [12288, 65536], P('row', ('col', 'depth')), may hold values from -0.0234375 to 0.0234375
- pair_energy: float32 [512], P(('col', 'depth')), may hold values from -4 to -1
- virt_energy: float32 [12288], P('row'), may hold values from 0.4 to 6
Outputs:
- residual: float32 [512, 12288], P(('col', 'depth'), 'row')
All inputs are finite; a program needn't handle non-finite values.
Results may differ from a plain program's by a relative error of at most 0.00011.
Values sent between devices are 32-bit elements; how exact they have to be, the bound alone decides.
No kernel may reach another device: no remote copies, remote signals or barrier semaphores. Data moves between devices by JAX's collectives and lax.ppermute only.
A program may use at most 128 MiB of HBM per device.

v0:
```python
import jax
import jax.numpy as jnp
from jax import lax
from jax.sharding import PartitionSpec as P


def tile_product(tile, integrals):
    return lax.dot_general(
        tile,
        integrals,
        (((1,), (1,)), ((), ())),
        precision=lax.Precision.HIGHEST,
        preferred_element_type=jnp.float32,
    )


def local(amplitudes, integrals, pair_energy, virt_energy):
    partial_sum = tile_product(lax.all_gather(amplitudes, "row", axis=0, tiled=True), integrals)
    ladder = lax.psum_scatter(partial_sum, ("col", "depth"), scatter_dimension=0, tiled=True)
    denominators = pair_energy[:, None] - virt_energy[None, :]
    return ladder / denominators


def solution(mesh):
    in_specs = (
        P("row", ("col", "depth")),
        P("row", ("col", "depth")),
        P(("col", "depth")),
        P("row"),
    )
    out_specs = P(("col", "depth"), "row")
    return jax.shard_map(local, mesh=mesh, in_specs=in_specs, out_specs=out_specs, check_vma=False)
```

profile of v0, /device:TPU:2, one launch (start us, length us, event | category | flops | bytes accessed | tf_op | source)
XLA Modules:
  0.0 240.1 jit_solution(470284990330593793)
XLA Ops:
  6.5 0.0 all-gather.2.cloned.1.call-start
  6.5 0.7 all-gather.2.cloned.1.call-update
  7.3 0.0 copy-start
  7.3 0.0 copy-start.1
  7.3 0.0 reduce-scatter.2.cloned.1.call-start
  7.3 140.5 %all-gather.2.cloned.1.call-done = f32[512,4096]{1,0:T(8,128)} async-done(((f32[32,4096]{1,0:T(8,128)}), f32[512,4096]{1,0:T(8,128)}) %all-gather.2.cloned.1.call-update) | async-done | bytes 8388624 | tf_op jit(solution)/shard_map/all_gather | solution.py:18
  147.8 24.9 %fusion = f32[512,768]{1,0:T(8,128)} fusion(f32[512,4096]{1,0:T(8,128)} %all-gather.2.cloned.1.call-done, f32[768,4096]{1,0:T(8,128)} %param.5), kind=kOutput, calls=%fused_computation.1 | convolution fusion | flops 19327352832 | bytes 22544384 | tf_op jit(solution)/shard_map/dot_general | solution.py:8
  172.7 0.0 reduce-scatter.2.cloned.1.call-update
  172.7 58.9 %reduce-scatter.2.cloned.1.call-done = f32[32,768]{1,0:T(8,128)} async-done(((f32[512,768]{1,0:T(8,128)}), f32[32,768]{1,0:T(8,128)}) %reduce-scatter.2.cloned.1.call-update) | async-done | bytes 98320 | tf_op jit(solution)/shard_map/reduce_scatter | solution.py:19
  231.7 0.0 copy-done
  231.7 0.0 copy-done.1
  231.7 1.6 subtract_divide_fusion
Async XLA Ops:
  6.5 141.3 %all-gather.2.cloned.1.call-start = ((), (), s32[]{:S(2)}) async-start(), calls=%async_computation.1 | async-start | bytes 8912896 | tf_op jit(solution)/shard_map/all_gather | solution.py:18
  7.3 224.4 %copy-start = (f32[768]{0:T(1024)S(1)}, f32[768]{0:T(1024)}, u32[]{:S(2)}) copy-start(f32[768]{0:T(1024)} %param.7) | copy-start | bytes 9220
  7.3 224.4 %copy-start.1 = (f32[32]{0:T(128)S(1)}, f32[32]{0:T(128)}, u32[]{:S(2)}) copy-start(f32[32]{0:T(128)} %param.6) | copy-start | bytes 388
  7.3 224.4 %reduce-scatter.2.cloned.1.call-start = ((), (), s32[]{:S(2)}) async-start(), calls=%async_computation.2 | async-start | bytes 1671168 | tf_op jit(solution)/shard_map/reduce_scatter | solution.py:19
Sparse Core Ops, SparseCore 0:
  9.9 137.8 all-gather.1
  172.9 58.7 reduce-scatter.1
where the time goes:
time: 244 us; the launch traced here: 240 us
  waiting for transfers between devices  200 us (82%)
  matrix products  24.9 us (10%)
  between operations  13.4 us (5%)
    all_gather x1, waiting for transfers between devices, local(): lax.all_gather(amplitudes, 'row', axis=0, tiled=True)  141 us
    reduce_scatter x1, waiting for transfers between devices, local(): lax.psum_scatter(partial_sum, ('col', 'depth'), scatter_dimension=0, tile...  58.9 us
    dot_general x1, matrix products, tile_product(): lax.dot_general(tile, integrals, (((1,), (1,)), ((), ())), precision=lax....  24.9 us
  transfers between devices with their start and end apart: 2, of which 2 were waited for; matrix products, arithmetic and copies ran while one was open for 0% of the time, Pallas kernels for 0%

commit v1 on v0

v1 whole, which is shorter than its diff:
```python
import functools

import jax
import jax.numpy as jnp
from jax import lax
from jax.experimental import pallas as pl
from jax.experimental.pallas import tpu as pltpu
from jax.sharding import PartitionSpec as P

NZ, NXH, NY, NXL = 8, 2, 4, 2
MIB = 1 << 20
VMEM = pl.BlockSpec(memory_space=pltpu.VMEM)
SMEM = pl.BlockSpec(memory_space=pltpu.SMEM)
HBM = pl.BlockSpec(memory_space=pltpu.HBM)
ANY = pl.BlockSpec(memory_space=pl.ANY)


def z_shift(block, step):
    perm = [(z * NXH + h, ((z + step) % NZ) * NXH + h) for z in range(NZ) for h in range(NXH)]
    return lax.ppermute(block, "row", perm)


def x_peer(block):
    perm = [(z * NXH + h, z * NXH + 1 - h) for z in range(NZ) for h in range(NXH)]
    return lax.ppermute(block, "row", perm)


def y_shift(block, step):
    perm = [(y * NXL + x, ((y + step) % NY) * NXL + x) for y in range(NY) for x in range(NXL)]
    return lax.ppermute(block, "col", perm)


def x_near(block):
    perm = [(y * NXL + x, y * NXL + 1 - x) for y in range(NY) for x in range(NXL)]
    return lax.ppermute(block, "col", perm)


def core_peer(block):
    return lax.ppermute(block, "depth", [(0, 1), (1, 0)])


def halves(values):
    high = values.astype(jnp.bfloat16)
    return high, (values - high.astype(jnp.float32)).astype(jnp.bfloat16)


def dot(a, b):
    return lax.dot_general(a, b, (((1,), (1,)), ((), ())), preferred_element_type=jnp.float32)


def group_kernel(plan, place, *refs, held):
    names = sorted({name for pieces in plan for name, *_ in pieces[2]})
    blocks = dict(zip(names, refs))
    high, low = refs[len(names) : len(names) + 2]
    out, token, left = refs[-3:]
    token[...] = jnp.zeros_like(token)
    total = left.shape[0] // 2
    at = 0
    for kind, d, pieces, start in plan:
        values = [blocks[name][first : first + count] for name, first, count in pieces]
        values = values[0] if len(values) == 1 else jnp.concatenate(values)
        count = values.shape[0]
        left[at : at + count], left[total + at : total + at + count] = halves(values)
        at += count
    z, flip = place[0], place[1]

    def tile(n, _):
        spot = pl.ds(pl.multiple_of(n * 256, 256), 256)
        both = dot(left[...], high[spot])
        sums = both[:total] + both[total:] + dot(left[:total], low[spot])
        at = 0
        for kind, d, pieces, start in plan:
            count = sum(p[2] for p in pieces)
            out[kind ^ flip, lax.rem(z + d + NZ, NZ), start : start + count, spot] = sums[at : at + count]
            at += count
        return 0

    lax.fori_loop(0, high.shape[0] // 256, tile, 0)


def group(plan, place, blocks, weights, partial, rows):
    names = sorted({name for pieces in plan for name, *_ in pieces[2]})
    columns, width = weights[0].shape
    total = sum(p[2] for _, _, pieces, _ in plan for p in pieces)
    operands = [place] + [blocks[name] for name in names] + list(weights)
    in_specs = [SMEM] + [VMEM] * (len(names) + 2)
    aliases = {}
    if partial is not None:
        aliases = {len(operands): 0}
        operands.append(partial)
        in_specs.append(VMEM)
    return pl.pallas_call(
        functools.partial(group_kernel, plan, held=partial is not None),
        out_shape=[
            jax.ShapeDtypeStruct((2, NZ, rows, columns), jnp.float32),
            jax.ShapeDtypeStruct((8, 128), jnp.float32),
        ],
        in_specs=in_specs,
        out_specs=[VMEM, VMEM],
        scratch_shapes=[pltpu.VMEM((2 * total, width), jnp.bfloat16)],
        input_output_aliases=aliases,
        compiler_params=pltpu.CompilerParams(vmem_limit_bytes=10 * MIB),
        cost_estimate=pl.CostEstimate(flops=4 * 3 * total * columns * width, bytes_accessed=MIB, transcendentals=0),
    )(*operands)


def first_kernel(plan, place, a0, up, down, peer, source, out, token, high, low, left, held, sems):
    steps, slots = 8, held.shape[0]
    count = source.shape[1] // steps

    def copy(step):
        slot = step % slots
        return pltpu.make_async_copy(source.at[:, pl.ds(step * count, count)], held.at[slot], sems.at[slot])

    for step in range(slots - 1):
        copy(step).start()
    token[...] = jnp.zeros_like(token)
    rows = a0.shape[0]
    total = 4 * rows
    for i, block in enumerate((a0, up, down, peer)):
        spot = pl.ds(i * rows, rows)
        left[spot], left[pl.ds(total + i * rows, rows)] = halves(block[...])
    z, flip = place[0], place[1]
    for step in range(steps):
        if step + slots - 1 < steps:
            copy(step + slots - 1).start()
        copy(step).wait()
        spot = pl.ds(step * count, count)
        high[:, spot], low[:, spot] = halves(held[step % slots])
        both = dot(left[:, spot], high[:, spot])
        sums = both[:total] + both[total:] + dot(left[:total, spot], low[:, spot])
        for i, (kind, d) in enumerate(plan):
            at = (kind ^ flip, lax.rem(z + d + NZ, NZ))
            part = sums[i * rows : (i + 1) * rows]
            out[at] = part if step == 0 else out[at] + part


def first_group(plan, place, blocks, integrals):
    rows, width = blocks[0].shape
    columns = integrals.shape[0]
    return pl.pallas_call(
        functools.partial(first_kernel, plan),
        out_shape=[
            jax.ShapeDtypeStruct((2, NZ, rows, columns), jnp.float32),
            jax.ShapeDtypeStruct((8, 128), jnp.float32),
            jax.ShapeDtypeStruct(integrals.shape, jnp.bfloat16),
            jax.ShapeDtypeStruct(integrals.shape, jnp.bfloat16),
        ],
        in_specs=[SMEM] + [VMEM] * 4 + [HBM],
        out_specs=[VMEM] * 4,
        scratch_shapes=[
            pltpu.VMEM((8 * rows, width), jnp.bfloat16),
            pltpu.VMEM((4, columns, width // 8), jnp.float32),
            pltpu.SemaphoreType.DMA((4,)),
        ],
        compiler_params=pltpu.CompilerParams(vmem_limit_bytes=40 * MIB),
        cost_estimate=pl.CostEstimate(flops=48 * rows * columns * width, bytes_accessed=12 * MIB, transcendentals=0),
    )(place, *blocks, integrals)


def stage_kernel(kept, cuts, *refs):
    inputs, outputs = refs[: len(refs) - kept - len(cuts)], refs[len(refs) - len(cuts) :]
    for out, parts in zip(outputs, cuts):
        at = 0
        for source, first, count in parts:
            out[at : at + count] = inputs[source][first : first + count]
            at += count


def stage(kept, others, cuts, weights, tokens):
    width = kept[0].shape[1]
    return pl.pallas_call(
        functools.partial(stage_kernel, len(kept), cuts),
        out_shape=[jax.ShapeDtypeStruct(v.shape, v.dtype) for v in kept]
        + [jax.ShapeDtypeStruct((sum(p[2] for p in parts), width), jnp.float32) for parts in cuts],
        in_specs=[VMEM] * (len(kept) + len(others) + len(weights)) + [ANY] * len(tokens),
        out_specs=[VMEM] * (len(kept) + len(cuts)),
        input_output_aliases={i: i for i in range(len(kept))},
        compiler_params=pltpu.CompilerParams(vmem_limit_bytes=4 * MIB),
        cost_estimate=pl.CostEstimate(flops=0, bytes_accessed=MIB, transcendentals=0),
    )(*kept, *others, *weights, *tokens)


def local(amplitudes, integrals, pair_energy, virt_energy):
    rows, width = amplitudes.shape
    columns = integrals.shape[0]
    half = rows // 2
    quarter = half // 2
    row, col, depth = (lax.axis_index(name) for name in ("row", "col", "depth"))
    z, h = row // NXH, row % NXH
    y, x = col // NXL, col % NXL
    place = jnp.stack([z, h ^ depth]).astype(jnp.int32)

    def ring(up, down):
        return z_shift(up, -1), z_shift(down, 1)

    def whole(kind, d, name):
        return (kind, d, ((name, 0, rows),), 0)

    def early(d, name):
        return (1, d, ((name, 0, half),), 0)

    def lates(d, name):
        return [(1, d, ((name, 0, half),), half), (1, -d, ((name, half, half),), half)]

    late = ((0, half, half), (1, half, half))
    a1 = ring(amplitudes, amplitudes)
    x0 = x_peer(amplitudes)
    *a1, b0, late1 = stage(a1, [x0], (((2, 0, half),), late), [], [])
    a2 = ring(*a1)
    b1 = ring(b0, b0)
    x1 = x_peer(late1)
    partial, token, *weights = first_group(
        ((0, 0), (0, 1), (0, -1), (1, 0)), place, [amplitudes, *a1, x0], integrals)
    b1 = stage(b1, [], (), weights, [token])
    b2 = ring(*b1)
    *a2, late2 = stage(a2, [], (late,), weights, b1)
    a3 = ring(*a2)
    x2 = x_peer(late2)
    partial, token = group(
        [whole(0, 2, "u"), whole(0, -2, "d"), *lates(1, "x"), early(1, "bu"), early(-1, "bd")],
        place, dict(u=a2[0], d=a2[1], x=x1, bu=b1[0], bd=b1[1]), weights, partial, rows)
    b2 = stage(b2, [], (), weights, [token])
    b3 = ring(*b2)
    *a3, up, down, late3 = stage(a3, [], (((0, 0, half),), ((1, half, half),), late), weights, b2)
    a4 = z_shift(up, -1), z_shift(down, 1)
    x3 = x_peer(late3)
    partial, token = group(
        [whole(0, 3, "u"), whole(0, -3, "d"), *lates(2, "x"), early(2, "bu"), early(-2, "bd")],
        place, dict(u=a3[0], d=a3[1], x=x2, bu=b2[0], bd=b2[1]), weights, partial, rows)
    *b3, up, down = stage(b3, [], (((0, 0, quarter),), ((1, quarter, quarter),)), weights, [token])
    b4 = z_shift(up, -1), z_shift(down, 1)
    x4 = x_peer(a4[1])
    partial, token = group(
        [
            (0, 4, (("a4u", 0, half), ("a4d", 0, half)), 0),
            early(3, "bu"),
            early(-3, "bd"),
            *lates(3, "x3"),
            (1, 4, (("b4u", 0, quarter), ("b4d", 0, quarter), ("x4", 0, half)), 0),
        ],
        place, dict(a4u=a4[0], a4d=a4[1], bu=b3[0], bd=b3[1], x3=x3, b4u=b4[0], b4d=b4[1], x4=x4), weights, partial, rows)

    total = (partial[0] + core_peer(partial[1])).reshape(NY, NXL, rows, columns)

    def at_y(value, step):
        return lax.dynamic_index_in_dim(value, (y + step) % NY, 0, keepdims=False)

    total = at_y(total, 0) + (y_shift(at_y(total, 2), 2) + y_shift(at_y(total, 1), 1) + y_shift(at_y(total, -1), -1))
    given = lax.dynamic_index_in_dim(total, 1 - x, 0, keepdims=False)
    total = lax.dynamic_index_in_dim(total, x, 0, keepdims=False) + x_near(given)
    return total / (pair_energy[:, None] - virt_energy[None, :])


def solution(mesh):
    in_specs = (
        P("row", ("col", "depth")),
        P("row", ("col", "depth")),
        P(("col", "depth")),
        P("row"),
    )
    out_specs = P(("col", "depth"), "row")
    return jax.shard_map(local, mesh=mesh, in_specs=in_specs, out_specs=out_specs, check_vma=False)
```

time: 244 us -> 112 us (0.46); the launches traced: 240 us -> 112 us
  waiting for transfers between devices: 200 us -> 40.7 us
  starting transfers between devices: 0.04 us -> 41.2 us
  Pallas kernels: 0 us -> 25.5 us
  matrix products: 24.9 us -> 0 us
  between operations: 13.4 us -> 0.26 us
  local copies, waits for them, and re-layouts: 0.01 us -> 2.93 us
    all_gather x1 -> x0, waiting for transfers between devices: 141 us -> none  [local(): lax.all_gather(amplitudes, 'row', axis=0, tiled=True)]
    reduce_scatter x1 -> x0, waiting for transfers between devices: 58.9 us -> none  [local(): lax.psum_scatter(partial_sum, ('col', 'depth'), scatter_dimension=0, tile...]
    ppermute x0 -> x26, starting transfers between devices: none -> 41.2 us  [the longest x16 25.2 us: z_shift(): return lax.ppermute(block, 'row', perm)]
    ppermute x0 -> x26, waiting for transfers between devices: none -> 40.7 us  [the longest x16 21.3 us: z_shift(): return lax.ppermute(block, 'row', perm)]
    pallas_call x0 -> x10, Pallas kernels: none -> 25.5 us  [the longest x3 15 us: group(): pl.pallas_call(functools.partial(group_kernel, plan, held=partial is not...]
    dot_general x1 -> x0, matrix products: 24.9 us -> none  [tile_product(): lax.dot_general(tile, integrals, (((1,), (1,)), ((), ())), precision=lax....]
    unnamed x4 -> x12, local copies, waits for them, and re-layouts: 0.01 us -> 2.81 us
  transfers between devices with their start and end apart: 2 -> 26, of which waited for: 2 -> 13; matrix products, arithmetic and copies ran while one was open for 0% -> 0% of each run, Pallas kernels for 0% -> 18%
where the time goes in v1:
time: 112 us
  starting transfers between devices  41.2 us (37%)
  waiting for transfers between devices  40.7 us (36%)
  Pallas kernels  25.5 us (23%)
  local copies, waits for them, and re-layouts  2.93 us (3%)
    ppermute x16, starting transfers between devices, z_shift(): return lax.ppermute(block, 'row', perm)  25.2 us
    ppermute x16, waiting for transfers between devices, z_shift(): return lax.ppermute(block, 'row', perm)  21.3 us
    pallas_call x3, Pallas kernels, group(): pl.pallas_call(functools.partial(group_kernel, plan, held=partial is not...  15 us
    pallas_call x1, Pallas kernels, first_group(): pl.pallas_call(functools.partial(first_kernel, plan), out_shape=[jax.Shap...  10.3 us
    ppermute x5, starting transfers between devices, x_peer(): return lax.ppermute(block, 'row', perm)  7.75 us
    ppermute x5, waiting for transfers between devices, x_peer(): return lax.ppermute(block, 'row', perm)  7.4 us
    ppermute x3, waiting for transfers between devices, y_shift(): return lax.ppermute(block, 'col', perm)  6.57 us
    ppermute x3, starting transfers between devices, y_shift(): return lax.ppermute(block, 'col', perm)  6.52 us
  transfers between devices with their start and end apart: 26, of which 13 were waited for; matrix products, arithmetic and copies ran while one was open for 0% of the time, Pallas kernels for 18%

profile of v1, /device:TPU:2, one launch (start us, length us, event | category | flops | bytes accessed | tf_op | source)
XLA Modules:
  0.0 111.5 jit_solution(6846033381839303418)
XLA Ops:
  0.0 2.1 %collective-permute-start.2 = (f32[32,4096]{1,0:T(8,128)}, f32[32,4096]{1,0:T(8,128)S(1)}, u32[]{:S(2)}, u32[]{:S(2)}) collective-permute-start(f32[32,4096]{1,0:T(8,128)} %a0.1), channel_id=1, source_target_pairs={{0,16},{16,0},{32,48},{48,32},{64,80},{80,64},{96,112},{112,96},{1... | collective-permute-start | bytes 1572872 | tf_op jit(solution)/shard_map/ppermute | solution.py:25
  2.1 5.9 %collective-permute-start = (f32[32,4096]{1,0:T(8,128)}, f32[32,4096]{1,0:T(8,128)S(1)}, u32[]{:S(2)}, u32[]{:S(2)}) collective-permute-start(f32[32,4096]{1,0:T(8,128)} %a0.1), channel_id=1, source_target_pairs={{0,224},{16,240},{32,0},{48,16},{64,32},{80,48},{96,64},{112,80},{... | collective-permute-start | bytes 1572872 | tf_op jit(solution)/shard_map/ppermute | solution.py:20
  8.0 7.4 %collective-permute-done.2.refs_2_.peer = f32[32,4096]{1,0:T(8,128)S(1)} collective-permute-done((f32[32,4096]{1,0:T(8,128)}, f32[32,4096]{1,0:T(8,128)S(1)}, u32[]{:S(2)}, u32[]{:S(2)}) %collective-permute-start.2) | collective-permute-done | bytes 524320 | tf_op jit(solution)/shard_map/ppermute | solution.py:25
  15.4 3.8 %collective-permute-done.refs_0_ = f32[32,4096]{1,0:T(8,128)S(1)} collective-permute-done((f32[32,4096]{1,0:T(8,128)}, f32[32,4096]{1,0:T(8,128)S(1)}, u32[]{:S(2)}, u32[]{:S(2)}) %collective-permute-start) | collective-permute-done | bytes 524320 | tf_op jit(solution)/shard_map/ppermute | solution.py:20
  19.2 3.3 %collective-permute-done.1.refs_1_ = f32[32,4096]{1,0:T(8,128)S(1)} collective-permute-done((f32[32,4096]{1,0:T(8,128)}, f32[32,4096]{1,0:T(8,128)S(1)}, u32[]{:S(2)}, u32[]{:S(2)}) %collective-permute-start.1) | collective-permute-done | bytes 524320 | tf_op jit(solution)/shard_map/ppermute | solution.py:20
  22.5 0.1 shard_map.46
  22.6 0.4 collective-permute-start.3
  22.9 1.7 %collective-permute-start.4 = (f32[32,4096]{1,0:T(8,128)S(1)}, f32[32,4096]{1,0:T(8,128)S(1)}, u32[]{:S(2)}, u32[]{:S(2)}) collective-permute-start(f32[32,4096]{1,0:T(8,128)S(1)} %get-tuple-element.35.down), channel_id=1, source_target_pairs={{0,32},{16,48},{32,64},{48,80},{64,96},{80,112},{96,128},{112,144}... | collective-permute-start | bytes 1572872 | tf_op jit(solution)/shard_map/ppermute | solution.py:20
  24.7 0.1 pad_add_fusion.place
  24.7 1.5 %collective-permute-start.5 = (f32[16,4096]{1,0:T(8,128)S(1)}, f32[16,4096]{1,0:T(8,128)S(1)}, u32[]{:S(2)}, u32[]{:S(2)}) collective-permute-start(f32[16,4096]{1,0:T(8,128)S(1)} %get-tuple-element.38), channel_id=1, source_target_pairs={{0,224},{16,240},{32,0},{48,16},{64,32},{80,48},{96,64},{112,80},{... | collective-permute-start | bytes 786440 | tf_op jit(solution)/shard_map/ppermute | solution.py:20
  26.2 0.5 collective-permute-start.6
  26.8 1.4 %collective-permute-start.11 = (f32[32,4096]{1,0:T(8,128)S(1)}, f32[32,4096]{1,0:T(8,128)S(1)}, u32[]{:S(2)}, u32[]{:S(2)}) collective-permute-start(f32[32,4096]{1,0:T(8,128)S(1)} %get-tuple-element.44), channel_id=1, source_target_pairs={{0,16},{16,0},{32,48},{48,32},{64,80},{80,64},{96,112},{112,96},{1... | collective-permute-start | bytes 1572872 | tf_op jit(solution)/shard_map/ppermute | solution.py:25
  28.2 10.3 %shard_map.47 = (f32[2,8,32,768]{3,2,1,0:T(8,128)S(1)}, f32[8,128]{1,0:T(8,128)S(1)}, bf16[768,4096]{1,0:T(8,128)(2,1)S(1)}, bf16[768,4096]{1,0:T(8,128)(2,1)}) custom-call(s32[2]{0:T(128)S(1)} %pad_add_fusion.place, f32[32,4096]{1,0:T(8,128)S(1)} %copy-done.1, f32[32,4096]{1,0:T(8,128)S(1)} %get-tuple-element.34.up, f32[32,4096]{1,0:T(8,128)S(1)} %get-tuple-element.35.down, ...), custom_call_target="tpu_custom_call" | custom-call | flops 4831838208 | bytes 12582912 | tf_op jit(solution)/shard_map/pallas_call | solution.py:141
  38.5 1.9 %collective-permute-done.5.refs_0_ = f32[16,4096]{1,0:T(8,128)S(1)} collective-permute-done((f32[16,4096]{1,0:T(8,128)S(1)}, f32[16,4096]{1,0:T(8,128)S(1)}, u32[]{:S(2)}, u32[]{:S(2)}) %collective-permute-start.5) | collective-permute-done | bytes 262176 | tf_op jit(solution)/shard_map/ppermute | solution.py:20
  40.4 1.5 %collective-permute-done.6.refs_1_ = f32[16,4096]{1,0:T(8,128)S(1)} collective-permute-done((f32[16,4096]{1,0:T(8,128)S(1)}, f32[16,4096]{1,0:T(8,128)S(1)}, u32[]{:S(2)}, u32[]{:S(2)}) %collective-permute-start.6) | collective-permute-done | bytes 262176 | tf_op jit(solution)/shard_map/ppermute | solution.py:20
  41.9 2.8 %copy-done = bf16[768,4096]{1,0:T(8,128)(2,1)S(1)} copy-done((bf16[768,4096]{1,0:T(8,128)(2,1)S(1)}, bf16[768,4096]{1,0:T(8,128)(2,1)}, u32[]{:S(2)}) %copy-start) | copy-done | bytes 6291480
  44.8 0.4 collective-permute-start.7
  45.2 1.7 %collective-permute-start.8 = (f32[32,4096]{1,0:T(8,128)S(1)}, f32[32,4096]{1,0:T(8,128)S(1)}, u32[]{:S(2)}, u32[]{:S(2)}) collective-permute-start(f32[32,4096]{1,0:T(8,128)S(1)} %get-tuple-element.43.refs_2_), channel_id=1, source_target_pairs={{0,32},{16,48},{32,64},{48,80},{64,96},{80,112},{96,128},{112,144}... | collective-permute-start | bytes 1572872 | tf_op jit(solution)/shard_map/ppermute | solution.py:20
  46.9 0.2 collective-permute-start.10
  47.1 3.0 %collective-permute-start.9 = (f32[16,4096]{1,0:T(8,128)S(1)}, f32[16,4096]{1,0:T(8,128)S(1)}, u32[]{:S(2)}, u32[]{:S(2)}) collective-permute-start(f32[16,4096]{1,0:T(8,128)S(1)} %get-tuple-element.40.refs_4_.refs_1_), channel_id=1, source_target_pairs={{0,224},{16,240},{32,0},{48,16},{64,32},{80,48},{96,64},{112,80},{... | collective-permute-start | bytes 786440 | tf_op jit(solution)/shard_map/ppermute | solution.py:20
  50.1 1.4 %collective-permute-start.16 = (f32[32,4096]{1,0:T(8,128)S(1)}, f32[32,4096]{1,0:T(8,128)S(1)}, u32[]{:S(2)}, u32[]{:S(2)}) collective-permute-start(f32[32,4096]{1,0:T(8,128)S(1)} %get-tuple-element.53), channel_id=1, source_target_pairs={{0,16},{16,0},{32,48},{48,32},{64,80},{80,64},{96,112},{112,96},{1... | collective-permute-start | bytes 1572872 | tf_op jit(solution)/shard_map/ppermute | solution.py:25
  51.6 4.8 %shard_map.50 = (f32[2,8,32,768]{3,2,1,0:T(8,128)S(1)}, f32[8,128]{1,0:T(8,128)S(1)}) custom-call(s32[2]{0:T(128)S(1)} %pad_add_fusion.place, f32[16,4096]{1,0:T(8,128)S(1)} %get-tuple-element.41.refs_5_.refs_0_, f32[16,4096]{1,0:T(8,128)S(1)} %get-tuple-element.40.refs_4_.refs_1_, ...), custom_call_target="tpu_custom_call", output_to_operand_aliasing={{0}: (8, {})} | custom-call | flops 4831838208 | bytes 1048576 | tf_op jit(solution)/shard_map/pallas_call | solution.py:92
  56.4 6.9 %collective-permute-done.10.refs_1_ = f32[16,4096]{1,0:T(8,128)S(1)} collective-permute-done((f32[16,4096]{1,0:T(8,128)S(1)}, f32[16,4096]{1,0:T(8,128)S(1)}, u32[]{:S(2)}, u32[]{:S(2)}) %collective-permute-start.10) | collective-permute-done | bytes 262176 | tf_op jit(solution)/shard_map/ppermute | solution.py:20
  63.3 0.1 shard_map.52
  63.4 0.9 collective-permute-start.12
  64.3 2.4 %collective-permute-start.14 = (f32[16,4096]{1,0:T(8,128)S(1)}, f32[16,4096]{1,0:T(8,128)S(1)}, u32[]{:S(2)}, u32[]{:S(2)}) collective-permute-start(f32[16,4096]{1,0:T(8,128)S(1)} %get-tuple-element.47.refs_4_.refs_1_), channel_id=1, source_target_pairs={{0,224},{16,240},{32,0},{48,16},{64,32},{80,48},{96,64},{112,80},{... | collective-permute-start | bytes 786440 | tf_op jit(solution)/shard_map/ppermute | solution.py:20
  66.7 1.4 %collective-permute-start.19 = (f32[32,4096]{1,0:T(8,128)S(1)}, f32[32,4096]{1,0:T(8,128)S(1)}, u32[]{:S(2)}, u32[]{:S(2)}) collective-permute-start(f32[32,4096]{1,0:T(8,128)S(1)} %get-tuple-element.60), channel_id=1, source_target_pairs={{0,16},{16,0},{32,48},{48,32},{64,80},{80,64},{96,112},{112,96},{1... | collective-permute-start | bytes 1572872 | tf_op jit(solution)/shard_map/ppermute | solution.py:25
  68.1 3.2 %collective-permute-start.13 = (f32[16,4096]{1,0:T(8,128)S(1)}, f32[16,4096]{1,0:T(8,128)S(1)}, u32[]{:S(2)}, u32[]{:S(2)}) collective-permute-start(f32[16,4096]{1,0:T(8,128)S(1)} %get-tuple-element.50), channel_id=1, source_target_pairs={{0,224},{16,240},{32,0},{48,16},{64,32},{80,48},{96,64},{112,80},{... | collective-permute-start | bytes 786440 | tf_op jit(solution)/shard_map/ppermute | solution.py:20
  71.3 0.9 collective-permute-done.12.refs_0_
  72.2 1.4 %collective-permute-start.20 = (f32[16,4096]{1,0:T(8,128)S(1)}, f32[16,4096]{1,0:T(8,128)S(1)}, u32[]{:S(2)}, u32[]{:S(2)}) collective-permute-start(f32[16,4096]{1,0:T(8,128)S(1)} %collective-permute-done.12.refs_0_), channel_id=1, source_target_pairs={{0,16},{16,0},{32,48},{48,32},{64,80},{80,64},{96,112},{112,96},{1... | collective-permute-start | bytes 786440 | tf_op jit(solution)/shard_map/ppermute | solution.py:25
  73.6 4.8 %shard_map.53 = (f32[2,8,32,768]{3,2,1,0:T(8,128)S(1)}, f32[8,128]{1,0:T(8,128)S(1)}) custom-call(s32[2]{0:T(128)S(1)} %pad_add_fusion.place, f32[16,4096]{1,0:T(8,128)S(1)} %get-tuple-element.48.refs_5_.refs_0_, f32[16,4096]{1,0:T(8,128)S(1)} %get-tuple-element.47.refs_4_.refs_1_, ...), custom_call_target="tpu_custom_call", output_to_operand_aliasing={{0}: (8, {})} | custom-call | flops 4831838208 | bytes 1048576 | tf_op jit(solution)/shard_map/pallas_call | solution.py:92
  78.5 0.1 collective-permute-start.17
  78.5 3.2 %collective-permute-start.18 = (f32[8,4096]{1,0:T(8,128)S(1)}, f32[8,4096]{1,0:T(8,128)S(1)}, u32[]{:S(2)}, u32[]{:S(2)}) collective-permute-start(f32[8,4096]{1,0:T(8,128)S(1)} %get-tuple-element.57), channel_id=1, source_target_pairs={{0,224},{16,240},{32,0},{48,16},{64,32},{80,48},{96,64},{112,80},{... | collective-permute-start | bytes 393224 | tf_op jit(solution)/shard_map/ppermute | solution.py:20
  81.8 2.9 %collective-permute-done.17.refs_2_ = f32[8,4096]{1,0:T(8,128)S(1)} collective-permute-done((f32[8,4096]{1,0:T(8,128)S(1)}, f32[8,4096]{1,0:T(8,128)S(1)}, u32[]{:S(2)}, u32[]{:S(2)}) %collective-permute-start.17) | collective-permute-done | bytes 131104 | tf_op jit(solution)/shard_map/ppermute | solution.py:20
  84.7 5.4 %shard_map.55 = (f32[2,8,32,768]{3,2,1,0:T(8,128)S(1)}, f32[8,128]{1,0:T(8,128)}) custom-call(s32[2]{0:T(128)S(1)} %pad_add_fusion.place, f32[16,4096]{1,0:T(8,128)S(1)} %collective-permute-done.12.refs_0_, f32[16,4096]{1,0:T(8,128)S(1)} %collective-permute-done.13.refs_1_, ...), custom_call_target="tpu_custom_call", output_to_operand_aliasing={{0}: (11, {})} | custom-call | flops 4831838208 | bytes 1048576 | tf_op jit(solution)/shard_map/pallas_call | solution.py:92
  90.1 0.1 slice_bitcast_fusion
  90.2 0.3 collective-permute-start.21
  90.6 2.2 %collective-permute-done.21 = f32[8,32,768]{2,1,0:T(8,128)S(1)} collective-permute-done((f32[8,32,768]{2,1,0:T(8,128)S(1)}, f32[8,32,768]{2,1,0:T(8,128)S(1)}, u32[]{:S(2)}, u32[]{:S(2)}) %collective-permute-start.21) | collective-permute-done | bytes 786464 | tf_op jit(solution)/shard_map/ppermute | solution.py:39
  92.8 0.1 bitcast_add_fusion
  92.9 3.3 %collective-permute-start.22 = (f32[2,32,768]{2,1,0:T(8,128)S(1)}, f32[2,32,768]{2,1,0:T(8,128)S(1)}, u32[]{:S(2)}, u32[]{:S(2)}) collective-permute-start(f32[2,32,768]{2,1,0:T(8,128)S(1)} %get-tuple-element.65), channel_id=1, source_target_pairs={{0,8},{2,10},{4,12},{6,14},{8,0},{10,2},{12,4},{14,6},{1,9},{3,11}... | collective-permute-start | bytes 589832 | tf_op jit(solution)/shard_map/ppermute | solution.py:30
  96.2 0.7 collective-permute-start.23
  96.9 2.6 %collective-permute-start.24 = (f32[2,32,768]{2,1,0:T(8,128)S(1)}, f32[2,32,768]{2,1,0:T(8,128)S(1)}, u32[]{:S(2)}, u32[]{:S(2)}) collective-permute-start(f32[2,32,768]{2,1,0:T(8,128)S(1)} %get-tuple-element.64), channel_id=1, source_target_pairs={{0,12},{2,14},{4,0},{6,2},{8,4},{10,6},{12,8},{14,10},{1,13},{3,15... | collective-permute-start | bytes 589832 | tf_op jit(solution)/shard_map/ppermute | solution.py:30
  99.5 2.8 %collective-permute-done.22 = f32[2,32,768]{2,1,0:T(8,128)S(1)} collective-permute-done((f32[2,32,768]{2,1,0:T(8,128)S(1)}, f32[2,32,768]{2,1,0:T(8,128)S(1)}, u32[]{:S(2)}, u32[]{:S(2)}) %collective-permute-start.22) | collective-permute-done | bytes 196640 | tf_op jit(solution)/shard_map/ppermute | solution.py:30
  102.3 3.4 %collective-permute-done.23 = f32[2,32,768]{2,1,0:T(8,128)S(1)} collective-permute-done((f32[2,32,768]{2,1,0:T(8,128)S(1)}, f32[2,32,768]{2,1,0:T(8,128)S(1)}, u32[]{:S(2)}, u32[]{:S(2)}) %collective-permute-start.23) | collective-permute-done | bytes 196640 | tf_op jit(solution)/shard_map/ppermute | solution.py:30
  105.7 0.3 collective-permute-done.24
  106.1 1.4 %collective-permute-start.25 = (f32[32,768]{1,0:T(8,128)S(1)}, f32[32,768]{1,0:T(8,128)S(1)}, u32[]{:S(2)}, u32[]{:S(2)}) collective-permute-start(f32[32,768]{1,0:T(8,128)S(1)} %dynamic-slice_bitcast_fusion.3), channel_id=1, source_target_pairs={{0,2},{2,0},{4,6},{6,4},{8,10},{10,8},{12,14},{14,12},{1,3},{3,1},... | collective-permute-start | bytes 294920 | tf_op jit(solution)/shard_map/ppermute | solution.py:35
  107.5 3.3 %collective-permute-done.25 = f32[32,768]{1,0:T(8,128)S(1)} collective-permute-done((f32[32,768]{1,0:T(8,128)S(1)}, f32[32,768]{1,0:T(8,128)S(1)}, u32[]{:S(2)}, u32[]{:S(2)}) %collective-permute-start.25) | collective-permute-done | bytes 98336 | tf_op jit(solution)/shard_map/ppermute | solution.py:35
  110.8 0.7 fusion
  (34 shorter events, 0.2 us)
Async XLA Ops:
  0.0 15.4 %collective-permute-start.2 = (f32[32,4096]{1,0:T(8,128)}, f32[32,4096]{1,0:T(8,128)S(1)}, u32[]{:S(2)}, u32[]{:S(2)}) collective-permute-start(f32[32,4096]{1,0:T(8,128)} %a0.1), channel_id=1, source_target_pairs={{0,16},{16,0},{32,48},{48,32},{64,80},{80,64},{96,112},{112,96},{1... | collective-permute-start | bytes 1572872 | tf_op jit(solution)/shard_map/ppermute | solution.py:25
  2.1 17.1 %collective-permute-start = (f32[32,4096]{1,0:T(8,128)}, f32[32,4096]{1,0:T(8,128)S(1)}, u32[]{:S(2)}, u32[]{:S(2)}) collective-permute-start(f32[32,4096]{1,0:T(8,128)} %a0.1), channel_id=1, source_target_pairs={{0,224},{16,240},{32,0},{48,16},{64,32},{80,48},{96,64},{112,80},{... | collective-permute-start | bytes 1572872 | tf_op jit(solution)/shard_map/ppermute | solution.py:20
  8.0 14.5 %collective-permute-start.1 = (f32[32,4096]{1,0:T(8,128)}, f32[32,4096]{1,0:T(8,128)S(1)}, u32[]{:S(2)}, u32[]{:S(2)}) collective-permute-start(f32[32,4096]{1,0:T(8,128)} %a0.1), channel_id=1, source_target_pairs={{0,32},{16,48},{32,64},{48,80},{64,96},{80,112},{96,128},{112,144}... | collective-permute-start | bytes 1572872 | tf_op jit(solution)/shard_map/ppermute | solution.py:20
  8.0 20.2 %copy-start.1 = (f32[32,4096]{1,0:T(8,128)S(1)}, f32[32,4096]{1,0:T(8,128)}, u32[]{:S(2)}) copy-start(f32[32,4096]{1,0:T(8,128)} %a0.1) | copy-start | bytes 1572868
  22.6 22.2 %collective-permute-start.3 = (f32[32,4096]{1,0:T(8,128)S(1)}, f32[32,4096]{1,0:T(8,128)S(1)}, u32[]{:S(2)}, u32[]{:S(2)}) collective-permute-start(f32[32,4096]{1,0:T(8,128)S(1)} %get-tuple-element.34.up), channel_id=1, source_target_pairs={{0,224},{16,240},{32,0},{48,16},{64,32},{80,48},{96,64},{112,80},{... | collective-permute-start | bytes 1572872 | tf_op jit(solution)/shard_map/ppermute | solution.py:20
  22.9 21.8 %collective-permute-start.4 = (f32[32,4096]{1,0:T(8,128)S(1)}, f32[32,4096]{1,0:T(8,128)S(1)}, u32[]{:S(2)}, u32[]{:S(2)}) collective-permute-start(f32[32,4096]{1,0:T(8,128)S(1)} %get-tuple-element.35.down), channel_id=1, source_target_pairs={{0,32},{16,48},{32,64},{48,80},{64,96},{80,112},{96,128},{112,144}... | collective-permute-start | bytes 1572872 | tf_op jit(solution)/shard_map/ppermute | solution.py:20
  24.7 15.7 %collective-permute-start.5 = (f32[16,4096]{1,0:T(8,128)S(1)}, f32[16,4096]{1,0:T(8,128)S(1)}, u32[]{:S(2)}, u32[]{:S(2)}) collective-permute-start(f32[16,4096]{1,0:T(8,128)S(1)} %get-tuple-element.38), channel_id=1, source_target_pairs={{0,224},{16,240},{32,0},{48,16},{64,32},{80,48},{96,64},{112,80},{... | collective-permute-start | bytes 786440 | tf_op jit(solution)/shard_map/ppermute | solution.py:20
  26.2 15.7 %collective-permute-start.6 = (f32[16,4096]{1,0:T(8,128)S(1)}, f32[16,4096]{1,0:T(8,128)S(1)}, u32[]{:S(2)}, u32[]{:S(2)}) collective-permute-start(f32[16,4096]{1,0:T(8,128)S(1)} %get-tuple-element.38), channel_id=1, source_target_pairs={{0,32},{16,48},{32,64},{48,80},{64,96},{80,112},{96,128},{112,144}... | collective-permute-start | bytes 786440 | tf_op jit(solution)/shard_map/ppermute | solution.py:20
  26.8 23.4 %collective-permute-start.11 = (f32[32,4096]{1,0:T(8,128)S(1)}, f32[32,4096]{1,0:T(8,128)S(1)}, u32[]{:S(2)}, u32[]{:S(2)}) collective-permute-start(f32[32,4096]{1,0:T(8,128)S(1)} %get-tuple-element.44), channel_id=1, source_target_pairs={{0,16},{16,0},{32,48},{48,32},{64,80},{80,64},{96,112},{112,96},{1... | collective-permute-start | bytes 1572872 | tf_op jit(solution)/shard_map/ppermute | solution.py:25
  41.9 2.8 %copy-start = (bf16[768,4096]{1,0:T(8,128)(2,1)S(1)}, bf16[768,4096]{1,0:T(8,128)(2,1)}, u32[]{:S(2)}) copy-start(bf16[768,4096]{1,0:T(8,128)(2,1)} %get-tuple-element.37.refs_3_.refs_6_.refs_9_) | copy-start | bytes 18874372
  44.7 6.8 %slice-start = ((s8[6291456]{0:T(1024)(128)(4,1)}), s8[4194304]{0:T(1024)(128)(4,1)S(1)}, s32[]{:S(2)}) async-start(s8[6291456]{0:T(1024)(128)(4,1)} %bitcast.21), calls=%async_computation | async-start | bytes 8388608
  44.7 6.8 %slice-start.1 = ((s8[6291456]{0:T(1024)(128)(4,1)}), s8[2097152]{0:T(1024)(128)(4,1)S(1)}, s32[]{:S(2)}) async-start(s8[6291456]{0:T(1024)(128)(4,1)} %bitcast.21), calls=%async_computation.1 | async-start | bytes 4194304
  44.8 18.5 %collective-permute-start.7 = (f32[32,4096]{1,0:T(8,128)S(1)}, f32[32,4096]{1,0:T(8,128)S(1)}, u32[]{:S(2)}, u32[]{:S(2)}) collective-permute-start(f32[32,4096]{1,0:T(8,128)S(1)} %get-tuple-element.42.refs_3_), channel_id=1, source_target_pairs={{0,224},{16,240},{32,0},{48,16},{64,32},{80,48},{96,64},{112,80},{... | collective-permute-start | bytes 1572872 | tf_op jit(solution)/shard_map/ppermute | solution.py:20
  45.2 18.1 %collective-permute-start.8 = (f32[32,4096]{1,0:T(8,128)S(1)}, f32[32,4096]{1,0:T(8,128)S(1)}, u32[]{:S(2)}, u32[]{:S(2)}) collective-permute-start(f32[32,4096]{1,0:T(8,128)S(1)} %get-tuple-element.43.refs_2_), channel_id=1, source_target_pairs={{0,32},{16,48},{32,64},{48,80},{64,96},{80,112},{96,128},{112,144}... | collective-permute-start | bytes 1572872 | tf_op jit(solution)/shard_map/ppermute | solution.py:20
  46.9 16.4 %collective-permute-start.10 = (f32[16,4096]{1,0:T(8,128)S(1)}, f32[16,4096]{1,0:T(8,128)S(1)}, u32[]{:S(2)}, u32[]{:S(2)}) collective-permute-start(f32[16,4096]{1,0:T(8,128)S(1)} %get-tuple-element.41.refs_5_.refs_0_), channel_id=1, source_target_pairs={{0,32},{16,48},{32,64},{48,80},{64,96},{80,112},{96,128},{112,144}... | collective-permute-start | bytes 786440 | tf_op jit(solution)/shard_map/ppermute | solution.py:20
  47.1 16.1 %collective-permute-start.9 = (f32[16,4096]{1,0:T(8,128)S(1)}, f32[16,4096]{1,0:T(8,128)S(1)}, u32[]{:S(2)}, u32[]{:S(2)}) collective-permute-start(f32[16,4096]{1,0:T(8,128)S(1)} %get-tuple-element.40.refs_4_.refs_1_), channel_id=1, source_target_pairs={{0,224},{16,240},{32,0},{48,16},{64,32},{80,48},{96,64},{112,80},{... | collective-permute-start | bytes 786440 | tf_op jit(solution)/shard_map/ppermute | solution.py:20
  50.1 17.9 %collective-permute-start.16 = (f32[32,4096]{1,0:T(8,128)S(1)}, f32[32,4096]{1,0:T(8,128)S(1)}, u32[]{:S(2)}, u32[]{:S(2)}) collective-permute-start(f32[32,4096]{1,0:T(8,128)S(1)} %get-tuple-element.53), channel_id=1, source_target_pairs={{0,16},{16,0},{32,48},{48,32},{64,80},{80,64},{96,112},{112,96},{1... | collective-permute-start | bytes 1572872 | tf_op jit(solution)/shard_map/ppermute | solution.py:25
  63.4 8.8 %collective-permute-start.12 = (f32[16,4096]{1,0:T(8,128)S(1)}, f32[16,4096]{1,0:T(8,128)S(1)}, u32[]{:S(2)}, u32[]{:S(2)}) collective-permute-start(f32[16,4096]{1,0:T(8,128)S(1)} %get-tuple-element.49), channel_id=1, source_target_pairs={{0,32},{16,48},{32,64},{48,80},{64,96},{80,112},{96,128},{112,144}... | collective-permute-start | bytes 786440 | tf_op jit(solution)/shard_map/ppermute | solution.py:20
  64.3 14.1 %collective-permute-start.14 = (f32[16,4096]{1,0:T(8,128)S(1)}, f32[16,4096]{1,0:T(8,128)S(1)}, u32[]{:S(2)}, u32[]{:S(2)}) collective-permute-start(f32[16,4096]{1,0:T(8,128)S(1)} %get-tuple-element.47.refs_4_.refs_1_), channel_id=1, source_target_pairs={{0,224},{16,240},{32,0},{48,16},{64,32},{80,48},{96,64},{112,80},{... | collective-permute-start | bytes 786440 | tf_op jit(solution)/shard_map/ppermute | solution.py:20
  66.7 11.7 %collective-permute-start.15 = (f32[16,4096]{1,0:T(8,128)S(1)}, f32[16,4096]{1,0:T(8,128)S(1)}, u32[]{:S(2)}, u32[]{:S(2)}) collective-permute-start(f32[16,4096]{1,0:T(8,128)S(1)} %get-tuple-element.48.refs_5_.refs_0_), channel_id=1, source_target_pairs={{0,32},{16,48},{32,64},{48,80},{64,96},{80,112},{96,128},{112,144}... | collective-permute-start | bytes 786440 | tf_op jit(solution)/shard_map/ppermute | solution.py:20
  66.7 18.1 %collective-permute-start.19 = (f32[32,4096]{1,0:T(8,128)S(1)}, f32[32,4096]{1,0:T(8,128)S(1)}, u32[]{:S(2)}, u32[]{:S(2)}) collective-permute-start(f32[32,4096]{1,0:T(8,128)S(1)} %get-tuple-element.60), channel_id=1, source_target_pairs={{0,16},{16,0},{32,48},{48,32},{64,80},{80,64},{96,112},{112,96},{1... | collective-permute-start | bytes 1572872 | tf_op jit(solution)/shard_map/ppermute | solution.py:25
  68.1 16.6 %collective-permute-start.13 = (f32[16,4096]{1,0:T(8,128)S(1)}, f32[16,4096]{1,0:T(8,128)S(1)}, u32[]{:S(2)}, u32[]{:S(2)}) collective-permute-start(f32[16,4096]{1,0:T(8,128)S(1)} %get-tuple-element.50), channel_id=1, source_target_pairs={{0,224},{16,240},{32,0},{48,16},{64,32},{80,48},{96,64},{112,80},{... | collective-permute-start | bytes 786440 | tf_op jit(solution)/shard_map/ppermute | solution.py:20
  72.2 12.5 %collective-permute-start.20 = (f32[16,4096]{1,0:T(8,128)S(1)}, f32[16,4096]{1,0:T(8,128)S(1)}, u32[]{:S(2)}, u32[]{:S(2)}) collective-permute-start(f32[16,4096]{1,0:T(8,128)S(1)} %collective-permute-done.12.refs_0_), channel_id=1, source_target_pairs={{0,16},{16,0},{32,48},{48,32},{64,80},{80,64},{96,112},{112,96},{1... | collective-permute-start | bytes 786440 | tf_op jit(solution)/shard_map/ppermute | solution.py:25
  78.5 6.3 %collective-permute-start.17 = (f32[8,4096]{1,0:T(8,128)S(1)}, f32[8,4096]{1,0:T(8,128)S(1)}, u32[]{:S(2)}, u32[]{:S(2)}) collective-permute-start(f32[8,4096]{1,0:T(8,128)S(1)} %get-tuple-element.56), channel_id=1, source_target_pairs={{0,32},{16,48},{32,64},{48,80},{64,96},{80,112},{96,128},{112,144}... | collective-permute-start | bytes 393224 | tf_op jit(solution)/shard_map/ppermute | solution.py:20
  78.5 6.2 %collective-permute-start.18 = (f32[8,4096]{1,0:T(8,128)S(1)}, f32[8,4096]{1,0:T(8,128)S(1)}, u32[]{:S(2)}, u32[]{:S(2)}) collective-permute-start(f32[8,4096]{1,0:T(8,128)S(1)} %get-tuple-element.57), channel_id=1, source_target_pairs={{0,224},{16,240},{32,0},{48,16},{64,32},{80,48},{96,64},{112,80},{... | collective-permute-start | bytes 393224 | tf_op jit(solution)/shard_map/ppermute | solution.py:20
  90.2 2.6 %collective-permute-start.21 = (f32[8,32,768]{2,1,0:T(8,128)S(1)}, f32[8,32,768]{2,1,0:T(8,128)S(1)}, u32[]{:S(2)}, u32[]{:S(2)}) collective-permute-start(f32[8,32,768]{2,1,0:T(8,128)S(1)} %slice_bitcast_fusion), channel_id=1, source_target_pairs={{0,1},{1,0},{2,3},{3,2},{4,5},{5,4},{6,7},{7,6},{8,9},{9,8},{10,11... | collective-permute-start | bytes 2359304 | tf_op jit(solution)/shard_map/ppermute | solution.py:39
  92.9 17.9 %copy-start.2 = (f32[768]{0:T(1024)S(1)}, f32[768]{0:T(1024)}, u32[]{:S(2)}) copy-start(f32[768]{0:T(1024)} %param.7) | copy-start | bytes 9220
  92.9 17.9 %copy-start.3 = (f32[32]{0:T(128)S(1)}, f32[32]{0:T(128)}, u32[]{:S(2)}) copy-start(f32[32]{0:T(128)} %param.6) | copy-start | bytes 388
  92.9 9.3 %collective-permute-start.22 = (f32[2,32,768]{2,1,0:T(8,128)S(1)}, f32[2,32,768]{2,1,0:T(8,128)S(1)}, u32[]{:S(2)}, u32[]{:S(2)}) collective-permute-start(f32[2,32,768]{2,1,0:T(8,128)S(1)} %get-tuple-element.65), channel_id=1, source_target_pairs={{0,8},{2,10},{4,12},{6,14},{8,0},{10,2},{12,4},{14,6},{1,9},{3,11}... | collective-permute-start | bytes 589832 | tf_op jit(solution)/shard_map/ppermute | solution.py:30
  96.2 9.5 %collective-permute-start.23 = (f32[2,32,768]{2,1,0:T(8,128)S(1)}, f32[2,32,768]{2,1,0:T(8,128)S(1)}, u32[]{:S(2)}, u32[]{:S(2)}) collective-permute-start(f32[2,32,768]{2,1,0:T(8,128)S(1)} %get-tuple-element.63), channel_id=1, source_target_pairs={{0,4},{2,6},{4,8},{6,10},{8,12},{10,14},{12,0},{14,2},{1,5},{3,7},... | collective-permute-start | bytes 589832 | tf_op jit(solution)/shard_map/ppermute | solution.py:30
  96.9 9.1 %collective-permute-start.24 = (f32[2,32,768]{2,1,0:T(8,128)S(1)}, f32[2,32,768]{2,1,0:T(8,128)S(1)}, u32[]{:S(2)}, u32[]{:S(2)}) collective-permute-start(f32[2,32,768]{2,1,0:T(8,128)S(1)} %get-tuple-element.64), channel_id=1, source_target_pairs={{0,12},{2,14},{4,0},{6,2},{8,4},{10,6},{12,8},{14,10},{1,13},{3,15... | collective-permute-start | bytes 589832 | tf_op jit(solution)/shard_map/ppermute | solution.py:30
  106.1 4.7 %collective-permute-start.25 = (f32[32,768]{1,0:T(8,128)S(1)}, f32[32,768]{1,0:T(8,128)S(1)}, u32[]{:S(2)}, u32[]{:S(2)}) collective-permute-start(f32[32,768]{1,0:T(8,128)S(1)} %dynamic-slice_bitcast_fusion.3), channel_id=1, source_target_pairs={{0,2},{2,0},{4,6},{6,4},{8,10},{10,8},{12,14},{14,12},{1,3},{3,1},... | collective-permute-start | bytes 294920 | tf_op jit(solution)/shard_map/ppermute | solution.py:35

commit v2 on v1

--- a/solution.py
+++ b/solution.py
@@ -25,13 +25,8 @@
     return lax.ppermute(block, "row", perm)
 
 
-def y_shift(block, step):
-    perm = [(y * NXL + x, ((y + step) % NY) * NXL + x) for y in range(NY) for x in range(NXL)]
-    return lax.ppermute(block, "col", perm)
-
-
-def x_near(block):
-    perm = [(y * NXL + x, y * NXL + 1 - x) for y in range(NY) for x in range(NXL)]
+def col_shift(block, dy, dx):
+    perm = [(y * NXL + x, ((y + dy) % NY) * NXL + (x ^ dx)) for y in range(NY) for x in range(NXL)]
     return lax.ppermute(block, "col", perm)
 
 
@@ -48,16 +43,24 @@
     return lax.dot_general(a, b, (((1,), (1,)), ((), ())), preferred_element_type=jnp.float32)
 
 
-def group_kernel(plan, place, *refs, held):
-    names = sorted({name for pieces in plan for name, *_ in pieces[2]})
+def names_of(plan):
+    return sorted({name for _, _, pieces, _ in plan for both, *_ in pieces for name in both.split()})
+
+
+def group_kernel(plan, place, *refs, held, first, adding):
+    names = names_of(plan)
     blocks = dict(zip(names, refs))
     high, low = refs[len(names) : len(names) + 2]
     out, token, left = refs[-3:]
+    span = pl.ds(first, left.shape[1])
     token[...] = jnp.zeros_like(token)
     total = left.shape[0] // 2
     at = 0
     for kind, d, pieces, start in plan:
-        values = [blocks[name][first : first + count] for name, first, count in pieces]
+        values = [
+            jnp.concatenate([blocks[name][low_row : low_row + count] for name in both.split()], axis=1)
+            for both, low_row, count in pieces
+        ]
         values = values[0] if len(values) == 1 else jnp.concatenate(values)
         count = values.shape[0]
         left[at : at + count], left[total + at : total + at + count] = halves(values)
@@ -65,22 +68,24 @@
     z, flip = place[0], place[1]
 
     def tile(n, _):
-        spot = pl.ds(pl.multiple_of(n * 256, 256), 256)
-        both = dot(left[...], high[spot])
-        sums = both[:total] + both[total:] + dot(left[:total], low[spot])
+        spot = pl.ds(pl.multiple_of(n * 768, 768), 768)
+        both = dot(left[...], high[spot, span])
+        sums = both[:total] + both[total:] + dot(left[:total], low[spot, span])
         at = 0
         for kind, d, pieces, start in plan:
             count = sum(p[2] for p in pieces)
-            out[kind ^ flip, lax.rem(z + d + NZ, NZ), start : start + count, spot] = sums[at : at + count]
+            where = (kind ^ flip, lax.rem(z + d + NZ, NZ), slice(start, start + count), spot)
+            out[where] = sums[at : at + count] + out[where] if adding else sums[at : at + count]
             at += count
         return 0
 
-    lax.fori_loop(0, high.shape[0] // 256, tile, 0)
-
-
-def group(plan, place, blocks, weights, partial, rows):
-    names = sorted({name for pieces in plan for name, *_ in pieces[2]})
-    columns, width = weights[0].shape
+    lax.fori_loop(0, high.shape[0] // 768, tile, 0)
+
+
+def group(plan, place, blocks, weights, partial, rows, first=0, adding=False):
+    names = names_of(plan)
+    columns = weights[0].shape[0]
+    width = max(block.shape[1] for block in blocks.values())
     total = sum(p[2] for _, _, pieces, _ in plan for p in pieces)
     operands = [place] + [blocks[name] for name in names] + list(weights)
     in_specs = [SMEM] + [VMEM] * (len(names) + 2)
@@ -90,7 +95,7 @@
         operands.append(partial)
         in_specs.append(VMEM)
     return pl.pallas_call(
-        functools.partial(group_kernel, plan, held=partial is not None),
+        functools.partial(group_kernel, plan, held=partial is not None, first=first, adding=adding),
         out_shape=[
             jax.ShapeDtypeStruct((2, NZ, rows, columns), jnp.float32),
             jax.ShapeDtypeStruct((8, 128), jnp.float32),
@@ -104,7 +109,7 @@
     )(*operands)
 
 
-def first_kernel(plan, place, a0, up, down, peer, source, out, token, high, low, left, held, sems):
+def first_kernel(plan, place, a0, source, out, token, high, low, left, held, sems):
     steps, slots = 8, held.shape[0]
     count = source.shape[1] // steps
 
@@ -116,8 +121,8 @@
         copy(step).start()
     token[...] = jnp.zeros_like(token)
     rows = a0.shape[0]
-    total = 4 * rows
-    for i, block in enumerate((a0, up, down, peer)):
+    total = rows
+    for i, block in enumerate((a0,)):
         spot = pl.ds(i * rows, rows)
         left[spot], left[pl.ds(total + i * rows, rows)] = halves(block[...])
     z, flip = place[0], place[1]
@@ -146,14 +151,14 @@
             jax.ShapeDtypeStruct(integrals.shape, jnp.bfloat16),
             jax.ShapeDtypeStruct(integrals.shape, jnp.bfloat16),
         ],
-        in_specs=[SMEM] + [VMEM] * 4 + [HBM],
+        in_specs=[SMEM, VMEM, HBM],
         out_specs=[VMEM] * 4,
         scratch_shapes=[
-            pltpu.VMEM((8 * rows, width), jnp.bfloat16),
+            pltpu.VMEM((2 * rows, width), jnp.bfloat16),
             pltpu.VMEM((4, columns, width // 8), jnp.float32),
             pltpu.SemaphoreType.DMA((4,)),
         ],
-        compiler_params=pltpu.CompilerParams(vmem_limit_bytes=40 * MIB),
+        compiler_params=pltpu.CompilerParams(vmem_limit_bytes=34 * MIB),
         cost_estimate=pl.CostEstimate(flops=48 * rows * columns * width, bytes_accessed=12 * MIB, transcendentals=0),
     )(place, *blocks, integrals)
 
@@ -162,17 +167,22 @@
     inputs, outputs = refs[: len(refs) - kept - len(cuts)], refs[len(refs) - len(cuts) :]
     for out, parts in zip(outputs, cuts):
         at = 0
-        for source, first, count in parts:
-            out[at : at + count] = inputs[source][first : first + count]
+        for source, first, count, *span in parts:
+            out[at : at + count] = inputs[source][first : first + count, slice(*(span or (None,)))]
             at += count
 
 
 def stage(kept, others, cuts, weights, tokens):
     width = kept[0].shape[1]
+
+    def shape(parts):
+        span = parts[0][3:] or (0, width)
+        return jax.ShapeDtypeStruct((sum(p[2] for p in parts), span[1] - span[0]), jnp.float32)
+
     return pl.pallas_call(
         functools.partial(stage_kernel, len(kept), cuts),
         out_shape=[jax.ShapeDtypeStruct(v.shape, v.dtype) for v in kept]
-        + [jax.ShapeDtypeStruct((sum(p[2] for p in parts), width), jnp.float32) for parts in cuts],
+        + [shape(parts) for parts in cuts],
         in_specs=[VMEM] * (len(kept) + len(others) + len(weights)) + [ANY] * len(tokens),
         out_specs=[VMEM] * (len(kept) + len(cuts)),
         input_output_aliases={i: i for i in range(len(kept))},
@@ -206,49 +216,48 @@
     late = ((0, half, half), (1, half, half))
     a1 = ring(amplitudes, amplitudes)
     x0 = x_peer(amplitudes)
-    *a1, b0, late1 = stage(a1, [x0], (((2, 0, half),), late), [], [])
+    partial, token, *weights = first_group(((0, 0),), place, [amplitudes], integrals)
+    *a1, b0, late1 = stage(a1, [x0], (((2, 0, half),), late), weights, [token])
     a2 = ring(*a1)
+    x1 = x_peer(late1)
+    partial, token = group(
+        [whole(0, 1, "u"), whole(0, -1, "d"), whole(1, 0, "x0")],
+        place, dict(u=a1[0], d=a1[1], x0=x0), weights, partial, rows)
+    (b0,) = stage([b0], [], (), weights, [token])
     b1 = ring(b0, b0)
-    x1 = x_peer(late1)
-    partial, token, *weights = first_group(
-        ((0, 0), (0, 1), (0, -1), (1, 0)), place, [amplitudes, *a1, x0], integrals)
-    b1 = stage(b1, [], (), weights, [token])
-    b2 = ring(*b1)
-    *a2, late2 = stage(a2, [], (late,), weights, b1)
+    *a2, late2 = stage(a2, [], (late,), weights, [x1])
     a3 = ring(*a2)
     x2 = x_peer(late2)
     partial, token = group(
         [whole(0, 2, "u"), whole(0, -2, "d"), *lates(1, "x"), early(1, "bu"), early(-1, "bd")],
         place, dict(u=a2[0], d=a2[1], x=x1, bu=b1[0], bd=b1[1]), weights, partial, rows)
-    b2 = stage(b2, [], (), weights, [token])
-    b3 = ring(*b2)
-    *a3, up, down, late3 = stage(a3, [], (((0, 0, half),), ((1, half, half),), late), weights, b2)
+    b1 = stage(b1, [], (), weights, [token])
+    b2 = ring(*b1)
+    *a3, up, down, late3 = stage(a3, [], (((0, 0, rows, 0, width // 2),), ((1, 0, rows, width // 2, width),), late), weights, [x2])
     a4 = z_shift(up, -1), z_shift(down, 1)
     x3 = x_peer(late3)
-    partial, token = group(
-        [whole(0, 3, "u"), whole(0, -3, "d"), *lates(2, "x"), early(2, "bu"), early(-2, "bd")],
-        place, dict(u=a3[0], d=a3[1], x=x2, bu=b2[0], bd=b2[1]), weights, partial, rows)
-    *b3, up, down = stage(b3, [], (((0, 0, quarter),), ((1, quarter, quarter),)), weights, [token])
-    b4 = z_shift(up, -1), z_shift(down, 1)
-    x4 = x_peer(a4[1])
+    b2 = stage(b2, [], (), weights, [late3])
+    b3 = ring(*b2)
+    x4 = x_peer(a4[0]), x_peer(a4[1])
     partial, token = group(
         [
-            (0, 4, (("a4u", 0, half), ("a4d", 0, half)), 0),
-            early(3, "bu"),
-            early(-3, "bd"),
-            *lates(3, "x3"),
-            (1, 4, (("b4u", 0, quarter), ("b4d", 0, quarter), ("x4", 0, half)), 0),
-        ],
-        place, dict(a4u=a4[0], a4d=a4[1], bu=b3[0], bd=b3[1], x3=x3, b4u=b4[0], b4d=b4[1], x4=x4), weights, partial, rows)
+            whole(0, 3, "a3u"), whole(0, -3, "a3d"), *lates(2, "x2"), early(2, "b2u"), early(-2, "b2d"),
+            (0, 4, (("a4u a4d", 0, rows),), 0), early(3, "b3u"), early(-3, "b3d"), *lates(3, "x3"),
+        ],
+        place,
+        dict(a3u=a3[0], a3d=a3[1], x2=x2, b2u=b2[0], b2d=b2[1], a4u=a4[0], a4d=a4[1], b3u=b3[0], b3d=b3[1], x3=x3),
+        weights, partial, rows)
+    partial, token = group([whole(1, 4, "y")], place, dict(y=x4[0]), weights, partial, rows)
+    partial, token = group([whole(1, 4, "y")], place, dict(y=x4[1]), weights, partial, rows, width // 2, True)
 
     total = (partial[0] + core_peer(partial[1])).reshape(NY, NXL, rows, columns)
 
-    def at_y(value, step):
-        return lax.dynamic_index_in_dim(value, (y + step) % NY, 0, keepdims=False)
-
-    total = at_y(total, 0) + (y_shift(at_y(total, 2), 2) + y_shift(at_y(total, 1), 1) + y_shift(at_y(total, -1), -1))
-    given = lax.dynamic_index_in_dim(total, 1 - x, 0, keepdims=False)
-    total = lax.dynamic_index_in_dim(total, x, 0, keepdims=False) + x_near(given)
+    def part(dy, dx):
+        at = ((y + dy) % NY, x ^ dx, 0, 0)
+        return lax.dynamic_slice(total, at, (1, 1, rows, columns)).reshape(rows, columns)
+
+    others = [(2, 1), (2, 0), (1, 1), (-1, 1), (1, 0), (-1, 0), (0, 1)]
+    total = sum((col_shift(part(*step), *step) for step in others), start=part(0, 0))
     return total / (pair_energy[:, None] - virt_energy[None, :])
 
 

time: 112 us -> 102 us (0.911)
  waiting for transfers between devices: 40.7 us -> 29.8 us
  Pallas kernels: 25.5 us -> 28.2 us
  local copies, waits for them, and re-layouts: 2.93 us -> 1.2 us
    ppermute x5 -> x6, waiting for transfers between devices: 7.4 us -> 0.02 us  [x_peer(): return lax.ppermute(block, 'row', perm)]
    ppermute x4 -> x7, waiting for transfers between devices: 9.86 us -> 4.05 us  [col_shift(): return lax.ppermute(block, 'col', perm)]
    ppermute x16 -> x14, starting transfers between devices: 25.2 us -> 19.5 us  [z_shift(): return lax.ppermute(block, 'row', perm)]
    pallas_call x3 -> x5, Pallas kernels: 15 us -> 20.6 us  [group(): pl.pallas_call(functools.partial(group_kernel, plan, held=partial is not...]
    ppermute x4 -> x7, starting transfers between devices: 7.93 us -> 12.6 us  [col_shift(): return lax.ppermute(block, 'col', perm)]
    pallas_call x1, Pallas kernels: 10.3 us -> 7.48 us  [first_group(): pl.pallas_call(functools.partial(first_kernel, plan), out_shape=[jax.Shap...]
    ppermute x16 -> x14, waiting for transfers between devices: 21.3 us -> 23.6 us  [z_shift(): return lax.ppermute(block, 'row', perm)]
    unnamed x12 -> x6, local copies, waits for them, and re-layouts: 2.81 us -> 1.08 us
  transfers between devices with their start and end apart: 26 -> 28, of which waited for: 13 -> 18; matrix products, arithmetic and copies ran while one was open for 0% -> 0% of each run, Pallas kernels for 18% -> 25%
where the time goes in v2:
time: 102 us
  starting transfers between devices  41.3 us (40%)
  waiting for transfers between devices  29.8 us (29%)
  Pallas kernels  28.2 us (28%)
  local copies, waits for them, and re-layouts  1.2 us (1%)
    ppermute x14, waiting for transfers between devices, z_shift(): return lax.ppermute(block, 'row', perm)  23.6 us
    pallas_call x5, Pallas kernels, group(): pl.pallas_call(functools.partial(group_kernel, plan, held=partial is not...  20.6 us
    ppermute x14, starting transfers between devices, z_shift(): return lax.ppermute(block, 'row', perm)  19.5 us
    ppermute x7, starting transfers between devices, col_shift(): return lax.ppermute(block, 'col', perm)  12.6 us
    ppermute x6, starting transfers between devices, x_peer(): return lax.ppermute(block, 'row', perm)  9.13 us
    pallas_call x1, Pallas kernels, first_group(): pl.pallas_call(functools.partial(first_kernel, plan), out_shape=[jax.Shap...  7.48 us
    ppermute x7, waiting for transfers between devices, col_shift(): return lax.ppermute(block, 'col', perm)  4.05 us
    ppermute x1, waiting for transfers between devices, core_peer(): return lax.ppermute(block, 'depth', [(0, 1), (1, 0)])  2.14 us
  transfers between devices with their start and end apart: 28, of which 18 were waited for; matrix products, arithmetic and copies ran while one was open for 0% of the time, Pallas kernels for 25%

profile of v2, /device:TPU:2, one launch (start us, length us, event | category | flops | bytes accessed | tf_op | source)
XLA Modules:
  0.0 101.7 jit_solution(9527458260539866040)
XLA Ops:
  0.0 2.1 %collective-permute-start.2 = (f32[32,4096]{1,0:T(8,128)}, f32[32,4096]{1,0:T(8,128)S(1)}, u32[]{:S(2)}, u32[]{:S(2)}) collective-permute-start(f32[32,4096]{1,0:T(8,128)} %a0.1), channel_id=1, source_target_pairs={{0,16},{16,0},{32,48},{48,32},{64,80},{80,64},{96,112},{112,96},{1... | collective-permute-start | bytes 1572872 | tf_op jit(solution)/shard_map/ppermute | solution.py:25
  2.1 5.9 %collective-permute-start = (f32[32,4096]{1,0:T(8,128)}, f32[32,4096]{1,0:T(8,128)S(1)}, u32[]{:S(2)}, u32[]{:S(2)}) collective-permute-start(f32[32,4096]{1,0:T(8,128)} %a0.1), channel_id=1, source_target_pairs={{0,224},{16,240},{32,0},{48,16},{64,32},{80,48},{96,64},{112,80},{... | collective-permute-start | bytes 1572872 | tf_op jit(solution)/shard_map/ppermute | solution.py:20
  8.1 1.1 %copy-done = f32[32,4096]{1,0:T(8,128)S(1)} copy-done((f32[32,4096]{1,0:T(8,128)S(1)}, f32[32,4096]{1,0:T(8,128)}, u32[]{:S(2)}) %copy-start) | copy-done | bytes 524312
  9.1 7.5 %shard_map.46 = (f32[2,8,32,768]{3,2,1,0:T(8,128)S(1)}, f32[8,128]{1,0:T(8,128)S(1)}, bf16[768,4096]{1,0:T(8,128)(2,1)S(1)}, bf16[768,4096]{1,0:T(8,128)(2,1)S(1)}) custom-call(s32[2]{0:T(128)S(1)} %pad_add_fusion.place, f32[32,4096]{1,0:T(8,128)S(1)} %copy-done, f32[768,4096]{1,0:T(8,128)} %source.1), custom_call_target="tpu_custom_call" | custom-call | flops 4831838208 | bytes 12582912 | tf_op jit(solution)/shard_map/pallas_call | solution.py:146
  16.6 2.6 %collective-permute-done.refs_0_ = f32[32,4096]{1,0:T(8,128)S(1)} collective-permute-done((f32[32,4096]{1,0:T(8,128)}, f32[32,4096]{1,0:T(8,128)S(1)}, u32[]{:S(2)}, u32[]{:S(2)}) %collective-permute-start) | collective-permute-done | bytes 524320 | tf_op jit(solution)/shard_map/ppermute | solution.py:20
  19.2 3.3 %collective-permute-done.1.refs_1_ = f32[32,4096]{1,0:T(8,128)S(1)} collective-permute-done((f32[32,4096]{1,0:T(8,128)}, f32[32,4096]{1,0:T(8,128)S(1)}, u32[]{:S(2)}, u32[]{:S(2)}) %collective-permute-start.1) | collective-permute-done | bytes 524320 | tf_op jit(solution)/shard_map/ppermute | solution.py:20
  22.6 0.4 collective-permute-start.3
  22.9 1.7 %collective-permute-start.4 = (f32[32,4096]{1,0:T(8,128)S(1)}, f32[32,4096]{1,0:T(8,128)S(1)}, u32[]{:S(2)}, u32[]{:S(2)}) collective-permute-start(f32[32,4096]{1,0:T(8,128)S(1)} %get-tuple-element.36.refs_0_), channel_id=1, source_target_pairs={{0,32},{16,48},{32,64},{48,80},{64,96},{80,112},{96,128},{112,144}... | collective-permute-start | bytes 1572872 | tf_op jit(solution)/shard_map/ppermute | solution.py:20
  24.7 1.4 %collective-permute-start.5 = (f32[32,4096]{1,0:T(8,128)S(1)}, f32[32,4096]{1,0:T(8,128)S(1)}, u32[]{:S(2)}, u32[]{:S(2)}) collective-permute-start(f32[32,4096]{1,0:T(8,128)S(1)} %get-tuple-element.37), channel_id=1, source_target_pairs={{0,16},{16,0},{32,48},{48,32},{64,80},{80,64},{96,112},{112,96},{1... | collective-permute-start | bytes 1572872 | tf_op jit(solution)/shard_map/ppermute | solution.py:25
  26.1 4.6 %shard_map.50 = (f32[2,8,32,768]{3,2,1,0:T(8,128)S(1)}, f32[8,128]{1,0:T(8,128)S(1)}) custom-call(s32[2]{0:T(128)S(1)} %pad_add_fusion.place, f32[32,4096]{1,0:T(8,128)S(1)} %get-tuple-element.36.refs_0_, f32[32,4096]{1,0:T(8,128)S(1)} %get-tuple-element.35.refs_1_, f32[32,4096]{1,0:T(8,128)S(1)} %collective-permute-done.2.refs_2_, ...), custom_call_target="tpu_custom_call", output_to_operand_aliasing={{0}: (6, {})} | custom-call | flops 3623878656 | bytes 1048576 | tf_op jit(solution)/shard_map/pallas_call | solution.py:97
  30.7 1.6 %collective-permute-start.13 = (f32[16,4096]{1,0:T(8,128)S(1)}, f32[16,4096]{1,0:T(8,128)S(1)}, u32[]{:S(2)}, u32[]{:S(2)}) collective-permute-start(f32[16,4096]{1,0:T(8,128)S(1)} %shard_map.51), channel_id=1, source_target_pairs={{0,224},{16,240},{32,0},{48,16},{64,32},{80,48},{96,64},{112,80},{... | collective-permute-start | bytes 786440 | tf_op jit(solution)/shard_map/ppermute | solution.py:20
  32.3 0.5 collective-permute-start.14
  32.8 4.7 %collective-permute-done.3.refs_0_ = f32[32,4096]{1,0:T(8,128)S(1)} collective-permute-done((f32[32,4096]{1,0:T(8,128)S(1)}, f32[32,4096]{1,0:T(8,128)S(1)}, u32[]{:S(2)}, u32[]{:S(2)}) %collective-permute-start.3) | collective-permute-done | bytes 524320 | tf_op jit(solution)/shard_map/ppermute | solution.py:20
  37.5 1.5 %collective-permute-done.4.refs_1_ = f32[32,4096]{1,0:T(8,128)S(1)} collective-permute-done((f32[32,4096]{1,0:T(8,128)S(1)}, f32[32,4096]{1,0:T(8,128)S(1)}, u32[]{:S(2)}, u32[]{:S(2)}) %collective-permute-start.4) | collective-permute-done | bytes 524320 | tf_op jit(solution)/shard_map/ppermute | solution.py:20
  39.0 0.7 collective-permute-start.6
  39.7 1.4 %collective-permute-start.7 = (f32[32,4096]{1,0:T(8,128)S(1)}, f32[32,4096]{1,0:T(8,128)S(1)}, u32[]{:S(2)}, u32[]{:S(2)}) collective-permute-start(f32[32,4096]{1,0:T(8,128)S(1)} %get-tuple-element.39.refs_2_), channel_id=1, source_target_pairs={{0,32},{16,48},{32,64},{48,80},{64,96},{80,112},{96,128},{112,144}... | collective-permute-start | bytes 1572872 | tf_op jit(solution)/shard_map/ppermute | solution.py:20
  41.1 0.7 collective-permute-start.8
  41.8 1.3 %collective-permute-done.13.refs_1_.refs_0_ = f32[16,4096]{1,0:T(8,128)S(1)} collective-permute-done((f32[16,4096]{1,0:T(8,128)S(1)}, f32[16,4096]{1,0:T(8,128)S(1)}, u32[]{:S(2)}, u32[]{:S(2)}) %collective-permute-start.13) | collective-permute-done | bytes 262176 | tf_op jit(solution)/shard_map/ppermute | solution.py:20
  43.1 0.3 collective-permute-done.14.refs_0_.refs_1_
  43.4 4.3 %shard_map.52 = (f32[2,8,32,768]{3,2,1,0:T(8,128)S(1)}, f32[8,128]{1,0:T(8,128)S(1)}) custom-call(s32[2]{0:T(128)S(1)} %pad_add_fusion.place, f32[16,4096]{1,0:T(8,128)S(1)} %collective-permute-done.14.refs_0_.refs_1_, f32[16,4096]{1,0:T(8,128)S(1)} %collective-permute-done.13.refs_1_.refs_0_, ...), custom_call_target="tpu_custom_call", output_to_operand_aliasing={{0}: (8, {})} | custom-call | flops 4831838208 | bytes 1048576 | tf_op jit(solution)/shard_map/pallas_call | solution.py:97
  47.7 1.0 collective-permute-start.15
  48.7 1.1 %collective-permute-start.16 = (f32[16,4096]{1,0:T(8,128)S(1)}, f32[16,4096]{1,0:T(8,128)S(1)}, u32[]{:S(2)}, u32[]{:S(2)}) collective-permute-start(f32[16,4096]{1,0:T(8,128)S(1)} %get-tuple-element.51), channel_id=1, source_target_pairs={{0,32},{16,48},{32,64},{48,80},{64,96},{80,112},{96,128},{112,144}... | collective-permute-start | bytes 786440 | tf_op jit(solution)/shard_map/ppermute | solution.py:20
  49.8 4.5 %collective-permute-done.6.refs_0_ = f32[32,4096]{1,0:T(8,128)S(1)} collective-permute-done((f32[32,4096]{1,0:T(8,128)S(1)}, f32[32,4096]{1,0:T(8,128)S(1)}, u32[]{:S(2)}, u32[]{:S(2)}) %collective-permute-start.6) | collective-permute-done | bytes 524320 | tf_op jit(solution)/shard_map/ppermute | solution.py:20
  54.4 1.4 %collective-permute-done.7.refs_1_ = f32[32,4096]{1,0:T(8,128)S(1)} collective-permute-done((f32[32,4096]{1,0:T(8,128)S(1)}, f32[32,4096]{1,0:T(8,128)S(1)}, u32[]{:S(2)}, u32[]{:S(2)}) %collective-permute-start.7) | collective-permute-done | bytes 524320 | tf_op jit(solution)/shard_map/ppermute | solution.py:20
  55.8 1.5 %collective-permute-start.19 = (f32[32,4096]{1,0:T(8,128)S(1)}, f32[32,4096]{1,0:T(8,128)S(1)}, u32[]{:S(2)}, u32[]{:S(2)}) collective-permute-start(f32[32,4096]{1,0:T(8,128)S(1)} %get-tuple-element.52.refs_4_), channel_id=1, source_target_pairs={{0,16},{16,0},{32,48},{48,32},{64,80},{80,64},{96,112},{112,96},{1... | collective-permute-start | bytes 1572872 | tf_op jit(solution)/shard_map/ppermute | solution.py:25
  57.3 2.0 %collective-permute-start.9 = (f32[32,2048]{1,0:T(8,128)S(1)}, f32[32,2048]{1,0:T(8,128)S(1)}, u32[]{:S(2)}, u32[]{:S(2)}) collective-permute-start(f32[32,2048]{1,0:T(8,128)S(1)} %get-tuple-element.41), channel_id=1, source_target_pairs={{0,32},{16,48},{32,64},{48,80},{64,96},{80,112},{96,128},{112,144}... | collective-permute-start | bytes 786440 | tf_op jit(solution)/shard_map/ppermute | solution.py:20
  59.4 0.6 collective-permute-done.15.refs_0_
  60.0 1.4 %collective-permute-done.16.refs_1_ = f32[16,4096]{1,0:T(8,128)S(1)} collective-permute-done((f32[16,4096]{1,0:T(8,128)S(1)}, f32[16,4096]{1,0:T(8,128)S(1)}, u32[]{:S(2)}, u32[]{:S(2)}) %collective-permute-start.16) | collective-permute-done | bytes 262176 | tf_op jit(solution)/shard_map/ppermute | solution.py:20
  61.7 2.9 %collective-permute-start.18 = (f32[16,4096]{1,0:T(8,128)S(1)}, f32[16,4096]{1,0:T(8,128)S(1)}, u32[]{:S(2)}, u32[]{:S(2)}) collective-permute-start(f32[16,4096]{1,0:T(8,128)S(1)} %get-tuple-element.54.refs_5_), channel_id=1, source_target_pairs={{0,224},{16,240},{32,0},{48,16},{64,32},{80,48},{96,64},{112,80},{... | collective-permute-start | bytes 786440 | tf_op jit(solution)/shard_map/ppermute | solution.py:20
  64.6 1.1 %collective-permute-done.11.refs_3_ = f32[32,2048]{1,0:T(8,128)S(1)} collective-permute-done((f32[32,2048]{1,0:T(8,128)S(1)}, f32[32,2048]{1,0:T(8,128)S(1)}, u32[]{:S(2)}, u32[]{:S(2)}) %collective-permute-start.11) | collective-permute-done | bytes 262176 | tf_op jit(solution)/shard_map/ppermute | solution.py:20
  65.7 1.4 %collective-permute-start.12 = (f32[32,2048]{1,0:T(8,128)S(1)}, f32[32,2048]{1,0:T(8,128)S(1)}, u32[]{:S(2)}, u32[]{:S(2)}) collective-permute-start(f32[32,2048]{1,0:T(8,128)S(1)} %collective-permute-done.11.refs_3_), channel_id=1, source_target_pairs={{0,16},{16,0},{32,48},{48,32},{64,80},{80,64},{96,112},{112,96},{1... | collective-permute-start | bytes 786440 | tf_op jit(solution)/shard_map/ppermute | solution.py:25
  67.2 2.0 %collective-permute-start.10 = (f32[32,2048]{1,0:T(8,128)S(1)}, f32[32,2048]{1,0:T(8,128)S(1)}, u32[]{:S(2)}, u32[]{:S(2)}) collective-permute-start(f32[32,2048]{1,0:T(8,128)S(1)} %collective-permute-done.9.refs_2_), channel_id=1, source_target_pairs={{0,16},{16,0},{32,48},{48,32},{64,80},{80,64},{96,112},{112,96},{1... | collective-permute-start | bytes 786440 | tf_op jit(solution)/shard_map/ppermute | solution.py:25
  69.3 0.8 collective-permute-done.17.refs_6_
  70.0 5.8 %shard_map.55 = (f32[2,8,32,768]{3,2,1,0:T(8,128)S(1)}, f32[8,128]{1,0:T(8,128)}) custom-call(s32[2]{0:T(128)S(1)} %pad_add_fusion.place, f32[32,4096]{1,0:T(8,128)S(1)} %get-tuple-element.43.refs_0_, f32[32,4096]{1,0:T(8,128)S(1)} %get-tuple-element.44.refs_1_, f32[32,2048]{1,0:T(8,128)S(1)} %collective-permute-done.9.refs_2_, ...), custom_call_target="tpu_custom_call", output_to_operand_aliasing={{0}: (13, {})} | custom-call | flops 8455716864 | bytes 1048576 | tf_op jit(solution)/shard_map/pallas_call | solution.py:97
  75.8 3.0 %shard_map.56 = (f32[2,8,32,768]{3,2,1,0:T(8,128)S(1)}, f32[8,128]{1,0:T(8,128)}) custom-call(s32[2]{0:T(128)S(1)} %pad_add_fusion.place, f32[32,2048]{1,0:T(8,128)S(1)} %collective-permute-done.12.refs_0_, bf16[768,4096]{1,0:T(8,128)(2,1)S(1)} %get-tuple-element.32.refs_3_.refs_2_.refs_1_.refs_5_.refs_10_, ...), custom_call_target="tpu_custom_call", output_to_operand_aliasing={{0}: (4, {})} | custom-call | flops 603979776 | bytes 1048576 | tf_op jit(solution)/shard_map/pallas_call | solution.py:97
  78.8 3.0 %shard_map.57 = (f32[2,8,32,768]{3,2,1,0:T(8,128)S(1)}, f32[8,128]{1,0:T(8,128)}) custom-call(s32[2]{0:T(128)S(1)} %pad_add_fusion.place, f32[32,2048]{1,0:T(8,128)S(1)} %collective-permute-done.10.refs_0_, bf16[768,4096]{1,0:T(8,128)(2,1)S(1)} %get-tuple-element.32.refs_3_.refs_2_.refs_1_.refs_5_.refs_10_, ...), custom_call_target="tpu_custom_call", output_to_operand_aliasing={{0}: (4, {})} | custom-call | flops 603979776 | bytes 1048576 | tf_op jit(solution)/shard_map/pallas_call | solution.py:97
  82.0 2.1 %collective-permute-done.20 = f32[8,32,768]{2,1,0:T(8,128)S(1)} collective-permute-done((f32[8,32,768]{2,1,0:T(8,128)S(1)}, f32[8,32,768]{2,1,0:T(8,128)S(1)}, u32[]{:S(2)}, u32[]{:S(2)}) %collective-permute-start.20) | collective-permute-done | bytes 786464 | tf_op jit(solution)/shard_map/ppermute | solution.py:34
  84.4 4.2 %collective-permute-start.21 = (f32[32,768]{1,0:T(8,128)S(1)}, f32[32,768]{1,0:T(8,128)S(1)}, u32[]{:S(2)}, u32[]{:S(2)}) collective-permute-start(f32[32,768]{1,0:T(8,128)S(1)} %get-tuple-element.59), channel_id=1, source_target_pairs={{0,10},{2,8},{4,14},{6,12},{8,2},{10,0},{12,6},{14,4},{1,11},{3,9}... | collective-permute-start | bytes 294920 | tf_op jit(solution)/shard_map/ppermute | solution.py:30
  88.5 0.3 collective-permute-start.22
  88.9 1.6 %collective-permute-start.23 = (f32[32,768]{1,0:T(8,128)S(1)}, f32[32,768]{1,0:T(8,128)S(1)}, u32[]{:S(2)}, u32[]{:S(2)}) collective-permute-start(f32[32,768]{1,0:T(8,128)S(1)} %get-tuple-element.64), channel_id=1, source_target_pairs={{0,6},{2,4},{4,10},{6,8},{8,14},{10,12},{12,2},{14,0},{1,7},{3,5},... | collective-permute-start | bytes 294920 | tf_op jit(solution)/shard_map/ppermute | solution.py:30
  90.5 2.5 %collective-permute-start.24 = (f32[32,768]{1,0:T(8,128)S(1)}, f32[32,768]{1,0:T(8,128)S(1)}, u32[]{:S(2)}, u32[]{:S(2)}) collective-permute-start(f32[32,768]{1,0:T(8,128)S(1)} %get-tuple-element.63), channel_id=1, source_target_pairs={{0,14},{2,12},{4,2},{6,0},{8,6},{10,4},{12,10},{14,8},{1,15},{3,13... | collective-permute-start | bytes 294920 | tf_op jit(solution)/shard_map/ppermute | solution.py:30
  93.0 0.4 collective-permute-start.25
  93.4 2.9 %collective-permute-start.26 = (f32[32,768]{1,0:T(8,128)S(1)}, f32[32,768]{1,0:T(8,128)S(1)}, u32[]{:S(2)}, u32[]{:S(2)}) collective-permute-start(f32[32,768]{1,0:T(8,128)S(1)} %get-tuple-element.61), channel_id=1, source_target_pairs={{0,12},{2,14},{4,0},{6,2},{8,4},{10,6},{12,8},{14,10},{1,13},{3,15... | collective-permute-start | bytes 294920 | tf_op jit(solution)/shard_map/ppermute | solution.py:30
  96.4 0.7 collective-permute-start.27
  97.1 0.3 collective-permute-done.24
  97.4 1.4 %collective-permute-done.25 = f32[32,768]{1,0:T(8,128)S(1)} collective-permute-done((f32[32,768]{1,0:T(8,128)S(1)}, f32[32,768]{1,0:T(8,128)S(1)}, u32[]{:S(2)}, u32[]{:S(2)}) %collective-permute-start.25) | collective-permute-done | bytes 98336 | tf_op jit(solution)/shard_map/ppermute | solution.py:30
  98.8 2.2 %collective-permute-done.27 = f32[32,768]{1,0:T(8,128)S(1)} collective-permute-done((f32[32,768]{1,0:T(8,128)S(1)}, f32[32,768]{1,0:T(8,128)S(1)}, u32[]{:S(2)}, u32[]{:S(2)}) %collective-permute-start.27) | collective-permute-done | bytes 98336 | tf_op jit(solution)/shard_map/ppermute | solution.py:30
  101.0 0.7 fusion.6
  (31 shorter events, 1.1 us)
Async XLA Ops:
  0.0 16.6 %collective-permute-start.2 = (f32[32,4096]{1,0:T(8,128)}, f32[32,4096]{1,0:T(8,128)S(1)}, u32[]{:S(2)}, u32[]{:S(2)}) collective-permute-start(f32[32,4096]{1,0:T(8,128)} %a0.1), channel_id=1, source_target_pairs={{0,16},{16,0},{32,48},{48,32},{64,80},{80,64},{96,112},{112,96},{1... | collective-permute-start | bytes 1572872 | tf_op jit(solution)/shard_map/ppermute | solution.py:25
  2.1 17.1 %collective-permute-start = (f32[32,4096]{1,0:T(8,128)}, f32[32,4096]{1,0:T(8,128)S(1)}, u32[]{:S(2)}, u32[]{:S(2)}) collective-permute-start(f32[32,4096]{1,0:T(8,128)} %a0.1), channel_id=1, source_target_pairs={{0,224},{16,240},{32,0},{48,16},{64,32},{80,48},{96,64},{112,80},{... | collective-permute-start | bytes 1572872 | tf_op jit(solution)/shard_map/ppermute | solution.py:20
  8.0 14.5 %collective-permute-start.1 = (f32[32,4096]{1,0:T(8,128)}, f32[32,4096]{1,0:T(8,128)S(1)}, u32[]{:S(2)}, u32[]{:S(2)}) collective-permute-start(f32[32,4096]{1,0:T(8,128)} %a0.1), channel_id=1, source_target_pairs={{0,32},{16,48},{32,64},{48,80},{64,96},{80,112},{96,128},{112,144}... | collective-permute-start | bytes 1572872 | tf_op jit(solution)/shard_map/ppermute | solution.py:20
  8.1 1.1 %copy-start = (f32[32,4096]{1,0:T(8,128)S(1)}, f32[32,4096]{1,0:T(8,128)}, u32[]{:S(2)}) copy-start(f32[32,4096]{1,0:T(8,128)} %a0.1) | copy-start | bytes 1572868
  22.6 14.9 %collective-permute-start.3 = (f32[32,4096]{1,0:T(8,128)S(1)}, f32[32,4096]{1,0:T(8,128)S(1)}, u32[]{:S(2)}, u32[]{:S(2)}) collective-permute-start(f32[32,4096]{1,0:T(8,128)S(1)} %get-tuple-element.35.refs_1_), channel_id=1, source_target_pairs={{0,224},{16,240},{32,0},{48,16},{64,32},{80,48},{96,64},{112,80},{... | collective-permute-start | bytes 1572872 | tf_op jit(solution)/shard_map/ppermute | solution.py:20
  22.9 16.1 %collective-permute-start.4 = (f32[32,4096]{1,0:T(8,128)S(1)}, f32[32,4096]{1,0:T(8,128)S(1)}, u32[]{:S(2)}, u32[]{:S(2)}) collective-permute-start(f32[32,4096]{1,0:T(8,128)S(1)} %get-tuple-element.36.refs_0_), channel_id=1, source_target_pairs={{0,32},{16,48},{32,64},{48,80},{64,96},{80,112},{96,128},{112,144}... | collective-permute-start | bytes 1572872 | tf_op jit(solution)/shard_map/ppermute | solution.py:20
  24.7 14.3 %collective-permute-start.5 = (f32[32,4096]{1,0:T(8,128)S(1)}, f32[32,4096]{1,0:T(8,128)S(1)}, u32[]{:S(2)}, u32[]{:S(2)}) collective-permute-start(f32[32,4096]{1,0:T(8,128)S(1)} %get-tuple-element.37), channel_id=1, source_target_pairs={{0,16},{16,0},{32,48},{48,32},{64,80},{80,64},{96,112},{112,96},{1... | collective-permute-start | bytes 1572872 | tf_op jit(solution)/shard_map/ppermute | solution.py:25
  30.7 12.4 %collective-permute-start.13 = (f32[16,4096]{1,0:T(8,128)S(1)}, f32[16,4096]{1,0:T(8,128)S(1)}, u32[]{:S(2)}, u32[]{:S(2)}) collective-permute-start(f32[16,4096]{1,0:T(8,128)S(1)} %shard_map.51), channel_id=1, source_target_pairs={{0,224},{16,240},{32,0},{48,16},{64,32},{80,48},{96,64},{112,80},{... | collective-permute-start | bytes 786440 | tf_op jit(solution)/shard_map/ppermute | solution.py:20
  32.3 11.2 %collective-permute-start.14 = (f32[16,4096]{1,0:T(8,128)S(1)}, f32[16,4096]{1,0:T(8,128)S(1)}, u32[]{:S(2)}, u32[]{:S(2)}) collective-permute-start(f32[16,4096]{1,0:T(8,128)S(1)} %shard_map.51), channel_id=1, source_target_pairs={{0,32},{16,48},{32,64},{48,80},{64,96},{80,112},{96,128},{112,144}... | collective-permute-start | bytes 786440 | tf_op jit(solution)/shard_map/ppermute | solution.py:20
  39.0 15.3 %collective-permute-start.6 = (f32[32,4096]{1,0:T(8,128)S(1)}, f32[32,4096]{1,0:T(8,128)S(1)}, u32[]{:S(2)}, u32[]{:S(2)}) collective-permute-start(f32[32,4096]{1,0:T(8,128)S(1)} %get-tuple-element.38.refs_3_), channel_id=1, source_target_pairs={{0,224},{16,240},{32,0},{48,16},{64,32},{80,48},{96,64},{112,80},{... | collective-permute-start | bytes 1572872 | tf_op jit(solution)/shard_map/ppermute | solution.py:20
  39.7 16.1 %collective-permute-start.7 = (f32[32,4096]{1,0:T(8,128)S(1)}, f32[32,4096]{1,0:T(8,128)S(1)}, u32[]{:S(2)}, u32[]{:S(2)}) collective-permute-start(f32[32,4096]{1,0:T(8,128)S(1)} %get-tuple-element.39.refs_2_), channel_id=1, source_target_pairs={{0,32},{16,48},{32,64},{48,80},{64,96},{80,112},{96,128},{112,144}... | collective-permute-start | bytes 1572872 | tf_op jit(solution)/shard_map/ppermute | solution.py:20
  41.1 14.6 %collective-permute-start.8 = (f32[32,4096]{1,0:T(8,128)S(1)}, f32[32,4096]{1,0:T(8,128)S(1)}, u32[]{:S(2)}, u32[]{:S(2)}) collective-permute-start(f32[32,4096]{1,0:T(8,128)S(1)} %get-tuple-element.40), channel_id=1, source_target_pairs={{0,16},{16,0},{32,48},{48,32},{64,80},{80,64},{96,112},{112,96},{1... | collective-permute-start | bytes 1572872 | tf_op jit(solution)/shard_map/ppermute | solution.py:25
  47.7 12.2 %collective-permute-start.15 = (f32[16,4096]{1,0:T(8,128)S(1)}, f32[16,4096]{1,0:T(8,128)S(1)}, u32[]{:S(2)}, u32[]{:S(2)}) collective-permute-start(f32[16,4096]{1,0:T(8,128)S(1)} %get-tuple-element.50), channel_id=1, source_target_pairs={{0,224},{16,240},{32,0},{48,16},{64,32},{80,48},{96,64},{112,80},{... | collective-permute-start | bytes 786440 | tf_op jit(solution)/shard_map/ppermute | solution.py:20
  48.7 12.7 %collective-permute-start.16 = (f32[16,4096]{1,0:T(8,128)S(1)}, f32[16,4096]{1,0:T(8,128)S(1)}, u32[]{:S(2)}, u32[]{:S(2)}) collective-permute-start(f32[16,4096]{1,0:T(8,128)S(1)} %get-tuple-element.51), channel_id=1, source_target_pairs={{0,32},{16,48},{32,64},{48,80},{64,96},{80,112},{96,128},{112,144}... | collective-permute-start | bytes 786440 | tf_op jit(solution)/shard_map/ppermute | solution.py:20
  55.8 14.2 %collective-permute-start.19 = (f32[32,4096]{1,0:T(8,128)S(1)}, f32[32,4096]{1,0:T(8,128)S(1)}, u32[]{:S(2)}, u32[]{:S(2)}) collective-permute-start(f32[32,4096]{1,0:T(8,128)S(1)} %get-tuple-element.52.refs_4_), channel_id=1, source_target_pairs={{0,16},{16,0},{32,48},{48,32},{64,80},{80,64},{96,112},{112,96},{1... | collective-permute-start | bytes 1572872 | tf_op jit(solution)/shard_map/ppermute | solution.py:25
  57.3 8.4 %collective-permute-start.11 = (f32[32,2048]{1,0:T(8,128)S(1)}, f32[32,2048]{1,0:T(8,128)S(1)}, u32[]{:S(2)}, u32[]{:S(2)}) collective-permute-start(f32[32,2048]{1,0:T(8,128)S(1)} %get-tuple-element.42), channel_id=1, source_target_pairs={{0,224},{16,240},{32,0},{48,16},{64,32},{80,48},{96,64},{112,80},{... | collective-permute-start | bytes 786440 | tf_op jit(solution)/shard_map/ppermute | solution.py:20
  57.3 9.9 %collective-permute-start.9 = (f32[32,2048]{1,0:T(8,128)S(1)}, f32[32,2048]{1,0:T(8,128)S(1)}, u32[]{:S(2)}, u32[]{:S(2)}) collective-permute-start(f32[32,2048]{1,0:T(8,128)S(1)} %get-tuple-element.41), channel_id=1, source_target_pairs={{0,32},{16,48},{32,64},{48,80},{64,96},{80,112},{96,128},{112,144}... | collective-permute-start | bytes 786440 | tf_op jit(solution)/shard_map/ppermute | solution.py:20
  61.4 8.6 %collective-permute-start.17 = (f32[16,4096]{1,0:T(8,128)S(1)}, f32[16,4096]{1,0:T(8,128)S(1)}, u32[]{:S(2)}, u32[]{:S(2)}) collective-permute-start(f32[16,4096]{1,0:T(8,128)S(1)} %get-tuple-element.53.refs_4_), channel_id=1, source_target_pairs={{0,32},{16,48},{32,64},{48,80},{64,96},{80,112},{96,128},{112,144}... | collective-permute-start | bytes 786440 | tf_op jit(solution)/shard_map/ppermute | solution.py:20
  61.7 8.3 %collective-permute-start.18 = (f32[16,4096]{1,0:T(8,128)S(1)}, f32[16,4096]{1,0:T(8,128)S(1)}, u32[]{:S(2)}, u32[]{:S(2)}) collective-permute-start(f32[16,4096]{1,0:T(8,128)S(1)} %get-tuple-element.54.refs_5_), channel_id=1, source_target_pairs={{0,224},{16,240},{32,0},{48,16},{64,32},{80,48},{96,64},{112,80},{... | collective-permute-start | bytes 786440 | tf_op jit(solution)/shard_map/ppermute | solution.py:20
  65.7 10.1 %collective-permute-start.12 = (f32[32,2048]{1,0:T(8,128)S(1)}, f32[32,2048]{1,0:T(8,128)S(1)}, u32[]{:S(2)}, u32[]{:S(2)}) collective-permute-start(f32[32,2048]{1,0:T(8,128)S(1)} %collective-permute-done.11.refs_3_), channel_id=1, source_target_pairs={{0,16},{16,0},{32,48},{48,32},{64,80},{80,64},{96,112},{112,96},{1... | collective-permute-start | bytes 786440 | tf_op jit(solution)/shard_map/ppermute | solution.py:25
  67.2 11.6 %collective-permute-start.10 = (f32[32,2048]{1,0:T(8,128)S(1)}, f32[32,2048]{1,0:T(8,128)S(1)}, u32[]{:S(2)}, u32[]{:S(2)}) collective-permute-start(f32[32,2048]{1,0:T(8,128)S(1)} %collective-permute-done.9.refs_2_), channel_id=1, source_target_pairs={{0,16},{16,0},{32,48},{48,32},{64,80},{80,64},{96,112},{112,96},{1... | collective-permute-start | bytes 786440 | tf_op jit(solution)/shard_map/ppermute | solution.py:25
  81.8 2.4 %collective-permute-start.20 = (f32[8,32,768]{2,1,0:T(8,128)S(1)}, f32[8,32,768]{2,1,0:T(8,128)S(1)}, u32[]{:S(2)}, u32[]{:S(2)}) collective-permute-start(f32[8,32,768]{2,1,0:T(8,128)S(1)} %slice_bitcast_fusion), channel_id=1, source_target_pairs={{0,1},{1,0},{2,3},{3,2},{4,5},{5,4},{6,7},{7,6},{8,9},{9,8},{10,11... | collective-permute-start | bytes 2359304 | tf_op jit(solution)/shard_map/ppermute | solution.py:34
  82.0 19.0 %copy-start.1 = (f32[768]{0:T(1024)S(1)}, f32[768]{0:T(1024)}, u32[]{:S(2)}) copy-start(f32[768]{0:T(1024)} %param.7) | copy-start | bytes 9220
  82.0 18.9 %copy-start.2 = (f32[32]{0:T(128)S(1)}, f32[32]{0:T(128)}, u32[]{:S(2)}) copy-start(f32[32]{0:T(128)} %param.6) | copy-start | bytes 388
  84.4 9.0 %collective-permute-start.21 = (f32[32,768]{1,0:T(8,128)S(1)}, f32[32,768]{1,0:T(8,128)S(1)}, u32[]{:S(2)}, u32[]{:S(2)}) collective-permute-start(f32[32,768]{1,0:T(8,128)S(1)} %get-tuple-element.59), channel_id=1, source_target_pairs={{0,10},{2,8},{4,14},{6,12},{8,2},{10,0},{12,6},{14,4},{1,11},{3,9}... | collective-permute-start | bytes 294920 | tf_op jit(solution)/shard_map/ppermute | solution.py:30
  88.5 7.8 %collective-permute-start.22 = (f32[32,768]{1,0:T(8,128)S(1)}, f32[32,768]{1,0:T(8,128)S(1)}, u32[]{:S(2)}, u32[]{:S(2)}) collective-permute-start(f32[32,768]{1,0:T(8,128)S(1)} %get-tuple-element.65), channel_id=1, source_target_pairs={{0,8},{2,10},{4,12},{6,14},{8,0},{10,2},{12,4},{14,6},{1,9},{3,11}... | collective-permute-start | bytes 294920 | tf_op jit(solution)/shard_map/ppermute | solution.py:30
  88.9 8.2 %collective-permute-start.23 = (f32[32,768]{1,0:T(8,128)S(1)}, f32[32,768]{1,0:T(8,128)S(1)}, u32[]{:S(2)}, u32[]{:S(2)}) collective-permute-start(f32[32,768]{1,0:T(8,128)S(1)} %get-tuple-element.64), channel_id=1, source_target_pairs={{0,6},{2,4},{4,10},{6,8},{8,14},{10,12},{12,2},{14,0},{1,7},{3,5},... | collective-permute-start | bytes 294920 | tf_op jit(solution)/shard_map/ppermute | solution.py:30
  90.5 6.9 %collective-permute-start.24 = (f32[32,768]{1,0:T(8,128)S(1)}, f32[32,768]{1,0:T(8,128)S(1)}, u32[]{:S(2)}, u32[]{:S(2)}) collective-permute-start(f32[32,768]{1,0:T(8,128)S(1)} %get-tuple-element.63), channel_id=1, source_target_pairs={{0,14},{2,12},{4,2},{6,0},{8,6},{10,4},{12,10},{14,8},{1,15},{3,13... | collective-permute-start | bytes 294920 | tf_op jit(solution)/shard_map/ppermute | solution.py:30
  93.0 5.8 %collective-permute-start.25 = (f32[32,768]{1,0:T(8,128)S(1)}, f32[32,768]{1,0:T(8,128)S(1)}, u32[]{:S(2)}, u32[]{:S(2)}) collective-permute-start(f32[32,768]{1,0:T(8,128)S(1)} %get-tuple-element.62), channel_id=1, source_target_pairs={{0,4},{2,6},{4,8},{6,10},{8,12},{10,14},{12,0},{14,2},{1,5},{3,7},... | collective-permute-start | bytes 294920 | tf_op jit(solution)/shard_map/ppermute | solution.py:30
  93.4 5.5 %collective-permute-start.26 = (f32[32,768]{1,0:T(8,128)S(1)}, f32[32,768]{1,0:T(8,128)S(1)}, u32[]{:S(2)}, u32[]{:S(2)}) collective-permute-start(f32[32,768]{1,0:T(8,128)S(1)} %get-tuple-element.61), channel_id=1, source_target_pairs={{0,12},{2,14},{4,0},{6,2},{8,4},{10,6},{12,8},{14,10},{1,13},{3,15... | collective-permute-start | bytes 294920 | tf_op jit(solution)/shard_map/ppermute | solution.py:30
  96.4 4.6 %collective-permute-start.27 = (f32[32,768]{1,0:T(8,128)S(1)}, f32[32,768]{1,0:T(8,128)S(1)}, u32[]{:S(2)}, u32[]{:S(2)}) collective-permute-start(f32[32,768]{1,0:T(8,128)S(1)} %get-tuple-element.60), channel_id=1, source_target_pairs={{0,2},{2,0},{4,6},{6,4},{8,10},{10,8},{12,14},{14,12},{1,3},{3,1},... | collective-permute-start | bytes 294920 | tf_op jit(solution)/shard_map/ppermute | solution.py:30

commit v3 on v2

--- a/solution.py
+++ b/solution.py
@@ -82,7 +82,7 @@
     lax.fori_loop(0, high.shape[0] // 768, tile, 0)
 
 
-def group(plan, place, blocks, weights, partial, rows, first=0, adding=False):
+def group(plan, place, blocks, weights, partial, rows, first=0, adding=False, lead=(2, NZ)):
     names = names_of(plan)
     columns = weights[0].shape[0]
     width = max(block.shape[1] for block in blocks.values())
@@ -97,7 +97,7 @@
     return pl.pallas_call(
         functools.partial(group_kernel, plan, held=partial is not None, first=first, adding=adding),
         out_shape=[
-            jax.ShapeDtypeStruct((2, NZ, rows, columns), jnp.float32),
+            jax.ShapeDtypeStruct((*lead, rows, columns), jnp.float32),
             jax.ShapeDtypeStruct((8, 128), jnp.float32),
         ],
         in_specs=in_specs,
@@ -126,6 +126,7 @@
         spot = pl.ds(i * rows, rows)
         left[spot], left[pl.ds(total + i * rows, rows)] = halves(block[...])
     z, flip = place[0], place[1]
+    out[1 ^ flip, lax.rem(z + NZ // 2, NZ)] = jnp.zeros(out.shape[2:], jnp.float32)
     for step in range(steps):
         if step + slots - 1 < steps:
             copy(step + slots - 1).start()
@@ -247,10 +248,14 @@
         place,
         dict(a3u=a3[0], a3d=a3[1], x2=x2, b2u=b2[0], b2d=b2[1], a4u=a4[0], a4d=a4[1], b3u=b3[0], b3d=b3[1], x3=x3),
         weights, partial, rows)
-    partial, token = group([whole(1, 4, "y")], place, dict(y=x4[0]), weights, partial, rows)
-    partial, token = group([whole(1, 4, "y")], place, dict(y=x4[1]), weights, partial, rows, width // 2, True)
-
-    total = (partial[0] + core_peer(partial[1])).reshape(NY, NXL, rows, columns)
+    total = partial[0] + core_peer(partial[1])
+    origin = jnp.zeros_like(place)
+    last, token = group([whole(0, 0, "y")], origin, dict(y=x4[0]), weights, None, rows, lead=(1, 1))
+    last, token = group([whole(0, 0, "y")], origin, dict(y=x4[1]), weights, last, rows, width // 2, True, (1, 1))
+    last = last[0, 0]
+    last = jnp.where(h ^ depth == 1, last + core_peer(last), 0.0)
+    far = (z + NZ // 2) % NZ == jnp.arange(NZ)
+    total = (total + jnp.where(far[:, None, None], last[None], 0.0)).reshape(NY, NXL, rows, columns)
 
     def part(dy, dx):
         at = ((y + dy) % NY, x ^ dx, 0, 0)

time: 102 us -> 122 us (1.20)
  waiting for transfers between devices: 29.8 us -> 37.8 us
  local copies, waits for them, and re-layouts: 1.2 us -> 6.75 us
  starting transfers between devices: 41.3 us -> 46.5 us
    ppermute x6, waiting for transfers between devices: 0.02 us -> 11.9 us  [x_peer(): return lax.ppermute(block, 'row', perm)]
    unnamed x6 -> x14, local copies, waits for them, and re-layouts: 1.08 us -> 6.63 us
    ppermute x14, waiting for transfers between devices: 23.6 us -> 20.3 us  [z_shift(): return lax.ppermute(block, 'row', perm)]
    ppermute x14, starting transfers between devices: 19.5 us -> 21.8 us  [z_shift(): return lax.ppermute(block, 'row', perm)]
    ppermute x7, starting transfers between devices: 12.6 us -> 14.1 us  [col_shift(): return lax.ppermute(block, 'col', perm)]
    ppermute x6, starting transfers between devices: 9.13 us -> 10.5 us  [x_peer(): return lax.ppermute(block, 'row', perm)]
  transfers between devices with their start and end apart: 28 -> 29, of which waited for: 18 -> 15; matrix products, arithmetic and copies ran while one was open for 0% -> 0% of each run, Pallas kernels for 25% -> 18%
where the time goes in v3:
time: 122 us; the launch traced here: 121 us
  starting transfers between devices  46.5 us (38%)
  waiting for transfers between devices  37.8 us (31%)
  Pallas kernels  28.2 us (23%)
  local copies, waits for them, and re-layouts  6.75 us (6%)
  other arithmetic  2.1 us (2%)
    ppermute x14, starting transfers between devices, z_shift(): return lax.ppermute(block, 'row', perm)  21.8 us
    pallas_call x5, Pallas kernels, group(): pl.pallas_call(functools.partial(group_kernel, plan, held=partial is not...  20.6 us
    ppermute x14, waiting for transfers between devices, z_shift(): return lax.ppermute(block, 'row', perm)  20.3 us
    ppermute x7, starting transfers between devices, col_shift(): return lax.ppermute(block, 'col', perm)  14.1 us
    ppermute x6, waiting for transfers between devices, x_peer(): return lax.ppermute(block, 'row', perm)  11.9 us
    ppermute x6, starting transfers between devices, x_peer(): return lax.ppermute(block, 'row', perm)  10.5 us
    pallas_call x1, Pallas kernels, first_group(): pl.pallas_call(functools.partial(first_kernel, plan), out_shape=[jax.Shap...  7.48 us
    unnamed x14, local copies, waits for them, and re-layouts  6.63 us
  transfers between devices with their start and end apart: 29, of which 15 were waited for; matrix products, arithmetic and copies ran while one was open for 0% of the time, Pallas kernels for 18%

profile of v3, /device:TPU:2, one launch (start us, length us, event | category | flops | bytes accessed | tf_op | source)
XLA Modules:
  0.0 121.5 jit_solution(3962308029790218839)
XLA Ops:
  0.0 1.9 %collective-permute-start.1 = (f32[32,4096]{1,0:T(8,128)}, f32[32,4096]{1,0:T(8,128)S(1)}, u32[]{:S(2)}, u32[]{:S(2)}) collective-permute-start(f32[32,4096]{1,0:T(8,128)} %a0.1), channel_id=1, source_target_pairs={{0,32},{16,48},{32,64},{48,80},{64,96},{80,112},{96,128},{112,144}... | collective-permute-start | bytes 1572872 | tf_op jit(solution)/shard_map/ppermute | solution.py:20
  1.9 3.9 %collective-permute-start = (f32[32,4096]{1,0:T(8,128)}, f32[32,4096]{1,0:T(8,128)S(1)}, u32[]{:S(2)}, u32[]{:S(2)}) collective-permute-start(f32[32,4096]{1,0:T(8,128)} %a0.1), channel_id=1, source_target_pairs={{0,224},{16,240},{32,0},{48,16},{64,32},{80,48},{96,64},{112,80},{... | collective-permute-start | bytes 1572872 | tf_op jit(solution)/shard_map/ppermute | solution.py:20
  5.9 2.1 %collective-permute-start.2 = (f32[32,4096]{1,0:T(8,128)}, f32[32,4096]{1,0:T(8,128)S(1)}, u32[]{:S(2)}, u32[]{:S(2)}) collective-permute-start(f32[32,4096]{1,0:T(8,128)} %a0.1), channel_id=1, source_target_pairs={{0,16},{16,0},{32,48},{48,32},{64,80},{80,64},{96,112},{112,96},{1... | collective-permute-start | bytes 1572872 | tf_op jit(solution)/shard_map/ppermute | solution.py:25
  8.1 1.0 copy-done.4
  9.1 7.5 %shard_map.46 = (f32[2,8,32,768]{3,2,1,0:T(8,128)S(1)}, f32[8,128]{1,0:T(8,128)S(1)}, bf16[768,4096]{1,0:T(8,128)(2,1)S(1)}, bf16[768,4096]{1,0:T(8,128)(2,1)S(1)}) custom-call(s32[2]{0:T(128)S(1)} %pad_add_fusion.place, f32[32,4096]{1,0:T(8,128)S(1)} %copy-done.4, f32[768,4096]{1,0:T(8,128)} %source.1), custom_call_target="tpu_custom_call" | custom-call | flops 4831838208 | bytes 12582912 | tf_op jit(solution)/shard_map/pallas_call | solution.py:147
  16.6 1.4 %collective-permute-done.1.refs_1_ = f32[32,4096]{1,0:T(8,128)S(1)} collective-permute-done((f32[32,4096]{1,0:T(8,128)}, f32[32,4096]{1,0:T(8,128)S(1)}, u32[]{:S(2)}, u32[]{:S(2)}) %collective-permute-start.1) | collective-permute-done | bytes 524320 | tf_op jit(solution)/shard_map/ppermute | solution.py:20
  18.0 3.0 %collective-permute-done.2.refs_2_ = f32[32,4096]{1,0:T(8,128)S(1)} collective-permute-done((f32[32,4096]{1,0:T(8,128)}, f32[32,4096]{1,0:T(8,128)S(1)}, u32[]{:S(2)}, u32[]{:S(2)}) %collective-permute-start.2) | collective-permute-done | bytes 524320 | tf_op jit(solution)/shard_map/ppermute | solution.py:25
  21.0 2.2 %collective-permute-start.5 = (f32[32,4096]{1,0:T(8,128)S(1)}, f32[32,4096]{1,0:T(8,128)S(1)}, u32[]{:S(2)}, u32[]{:S(2)}) collective-permute-start(f32[32,4096]{1,0:T(8,128)S(1)} %get-tuple-element.37), channel_id=1, source_target_pairs={{0,16},{16,0},{32,48},{48,32},{64,80},{80,64},{96,112},{112,96},{1... | collective-permute-start | bytes 1572872 | tf_op jit(solution)/shard_map/ppermute | solution.py:25
  23.2 1.7 %collective-permute-start.3 = (f32[32,4096]{1,0:T(8,128)S(1)}, f32[32,4096]{1,0:T(8,128)S(1)}, u32[]{:S(2)}, u32[]{:S(2)}) collective-permute-start(f32[32,4096]{1,0:T(8,128)S(1)} %get-tuple-element.35.refs_1_), channel_id=1, source_target_pairs={{0,224},{16,240},{32,0},{48,16},{64,32},{80,48},{96,64},{112,80},{... | collective-permute-start | bytes 1572872 | tf_op jit(solution)/shard_map/ppermute | solution.py:20
  25.0 0.3 collective-permute-start.4
  25.3 4.6 %shard_map.50 = (f32[2,8,32,768]{3,2,1,0:T(8,128)S(1)}, f32[8,128]{1,0:T(8,128)S(1)}) custom-call(s32[2]{0:T(128)S(1)} %pad_add_fusion.place, f32[32,4096]{1,0:T(8,128)S(1)} %get-tuple-element.36.refs_0_, f32[32,4096]{1,0:T(8,128)S(1)} %get-tuple-element.35.refs_1_, f32[32,4096]{1,0:T(8,128)S(1)} %collective-permute-done.2.refs_2_, ...), custom_call_target="tpu_custom_call", output_to_operand_aliasing={{0}: (6, {})} | custom-call | flops 3623878656 | bytes 1048576 | tf_op jit(solution)/shard_map/pallas_call | solution.py:97
  30.0 3.2 %collective-permute-start.11 = (f32[16,4096]{1,0:T(8,128)S(1)}, f32[16,4096]{1,0:T(8,128)S(1)}, u32[]{:S(2)}, u32[]{:S(2)}) collective-permute-start(f32[16,4096]{1,0:T(8,128)S(1)} %shard_map.51), channel_id=1, source_target_pairs={{0,224},{16,240},{32,0},{48,16},{64,32},{80,48},{96,64},{112,80},{... | collective-permute-start | bytes 786440 | tf_op jit(solution)/shard_map/ppermute | solution.py:20
  33.2 1.9 %collective-permute-done.5.refs_4_ = f32[32,4096]{1,0:T(8,128)S(1)} collective-permute-done((f32[32,4096]{1,0:T(8,128)S(1)}, f32[32,4096]{1,0:T(8,128)S(1)}, u32[]{:S(2)}, u32[]{:S(2)}) %collective-permute-start.5) | collective-permute-done | bytes 524320 | tf_op jit(solution)/shard_map/ppermute | solution.py:25
  35.1 3.0 %collective-permute-done.3.refs_0_ = f32[32,4096]{1,0:T(8,128)S(1)} collective-permute-done((f32[32,4096]{1,0:T(8,128)S(1)}, f32[32,4096]{1,0:T(8,128)S(1)}, u32[]{:S(2)}, u32[]{:S(2)}) %collective-permute-start.3) | collective-permute-done | bytes 524320 | tf_op jit(solution)/shard_map/ppermute | solution.py:20
  38.1 3.0 %collective-permute-done.4.refs_1_ = f32[32,4096]{1,0:T(8,128)S(1)} collective-permute-done((f32[32,4096]{1,0:T(8,128)S(1)}, f32[32,4096]{1,0:T(8,128)S(1)}, u32[]{:S(2)}, u32[]{:S(2)}) %collective-permute-start.4) | collective-permute-done | bytes 524320 | tf_op jit(solution)/shard_map/ppermute | solution.py:20
  41.1 1.1 collective-permute-start.8
  42.1 0.3 collective-permute-start.6
  42.4 1.7 %collective-permute-start.7 = (f32[32,4096]{1,0:T(8,128)S(1)}, f32[32,4096]{1,0:T(8,128)S(1)}, u32[]{:S(2)}, u32[]{:S(2)}) collective-permute-start(f32[32,4096]{1,0:T(8,128)S(1)} %get-tuple-element.39.refs_2_), channel_id=1, source_target_pairs={{0,32},{16,48},{32,64},{48,80},{64,96},{80,112},{96,128},{112,144}... | collective-permute-start | bytes 1572872 | tf_op jit(solution)/shard_map/ppermute | solution.py:20
  44.2 2.5 %collective-permute-done.12.refs_0_.refs_1_ = f32[16,4096]{1,0:T(8,128)S(1)} collective-permute-done((f32[16,4096]{1,0:T(8,128)S(1)}, f32[16,4096]{1,0:T(8,128)S(1)}, u32[]{:S(2)}, u32[]{:S(2)}) %collective-permute-start.12) | collective-permute-done | bytes 262176 | tf_op jit(solution)/shard_map/ppermute | solution.py:20
  46.7 4.3 %shard_map.52 = (f32[2,8,32,768]{3,2,1,0:T(8,128)S(1)}, f32[8,128]{1,0:T(8,128)S(1)}) custom-call(s32[2]{0:T(128)S(1)} %pad_add_fusion.place, f32[16,4096]{1,0:T(8,128)S(1)} %collective-permute-done.12.refs_0_.refs_1_, f32[16,4096]{1,0:T(8,128)S(1)} %collective-permute-done.11.refs_1_.refs_0_, ...), custom_call_target="tpu_custom_call", output_to_operand_aliasing={{0}: (8, {})} | custom-call | flops 4831838208 | bytes 1048576 | tf_op jit(solution)/shard_map/pallas_call | solution.py:97
  51.0 2.0 %collective-permute-start.14 = (f32[16,4096]{1,0:T(8,128)S(1)}, f32[16,4096]{1,0:T(8,128)S(1)}, u32[]{:S(2)}, u32[]{:S(2)}) collective-permute-start(f32[16,4096]{1,0:T(8,128)S(1)} %get-tuple-element.51), channel_id=1, source_target_pairs={{0,32},{16,48},{32,64},{48,80},{64,96},{80,112},{96,128},{112,144}... | collective-permute-start | bytes 786440 | tf_op jit(solution)/shard_map/ppermute | solution.py:20
  53.1 2.0 %collective-permute-done.6.refs_0_ = f32[32,4096]{1,0:T(8,128)S(1)} collective-permute-done((f32[32,4096]{1,0:T(8,128)S(1)}, f32[32,4096]{1,0:T(8,128)S(1)}, u32[]{:S(2)}, u32[]{:S(2)}) %collective-permute-start.6) | collective-permute-done | bytes 524320 | tf_op jit(solution)/shard_map/ppermute | solution.py:20
  55.1 2.4 %collective-permute-done.7.refs_1_ = f32[32,4096]{1,0:T(8,128)S(1)} collective-permute-done((f32[32,4096]{1,0:T(8,128)S(1)}, f32[32,4096]{1,0:T(8,128)S(1)}, u32[]{:S(2)}, u32[]{:S(2)}) %collective-permute-start.7) | collective-permute-done | bytes 524320 | tf_op jit(solution)/shard_map/ppermute | solution.py:20
  57.5 1.5 %collective-permute-start.17 = (f32[32,4096]{1,0:T(8,128)S(1)}, f32[32,4096]{1,0:T(8,128)S(1)}, u32[]{:S(2)}, u32[]{:S(2)}) collective-permute-start(f32[32,4096]{1,0:T(8,128)S(1)} %get-tuple-element.52.refs_4_), channel_id=1, source_target_pairs={{0,16},{16,0},{32,48},{48,32},{64,80},{80,64},{96,112},{112,96},{1... | collective-permute-start | bytes 1572872 | tf_op jit(solution)/shard_map/ppermute | solution.py:25
  59.0 1.2 %collective-permute-done.14.refs_1_ = f32[16,4096]{1,0:T(8,128)S(1)} collective-permute-done((f32[16,4096]{1,0:T(8,128)S(1)}, f32[16,4096]{1,0:T(8,128)S(1)}, u32[]{:S(2)}, u32[]{:S(2)}) %collective-permute-start.14) | collective-permute-done | bytes 262176 | tf_op jit(solution)/shard_map/ppermute | solution.py:20
  60.3 3.2 %collective-permute-start.16 = (f32[16,4096]{1,0:T(8,128)S(1)}, f32[16,4096]{1,0:T(8,128)S(1)}, u32[]{:S(2)}, u32[]{:S(2)}) collective-permute-start(f32[16,4096]{1,0:T(8,128)S(1)} %get-tuple-element.54.refs_5_), channel_id=1, source_target_pairs={{0,224},{16,240},{32,0},{48,16},{64,32},{80,48},{96,64},{112,80},{... | collective-permute-start | bytes 786440 | tf_op jit(solution)/shard_map/ppermute | solution.py:20
  63.5 3.2 %collective-permute-start.10 = (f32[32,2048]{1,0:T(8,128)S(1)}, f32[32,2048]{1,0:T(8,128)S(1)}, u32[]{:S(2)}, u32[]{:S(2)}) collective-permute-start(f32[32,2048]{1,0:T(8,128)S(1)} %get-tuple-element.44), channel_id=1, source_target_pairs={{0,224},{16,240},{32,0},{48,16},{64,32},{80,48},{96,64},{112,80},{... | collective-permute-start | bytes 786440 | tf_op jit(solution)/shard_map/ppermute | solution.py:20
  66.7 2.0 %collective-permute-done.15.refs_6_ = f32[16,4096]{1,0:T(8,128)S(1)} collective-permute-done((f32[16,4096]{1,0:T(8,128)S(1)}, f32[16,4096]{1,0:T(8,128)S(1)}, u32[]{:S(2)}, u32[]{:S(2)}) %collective-permute-start.15) | collective-permute-done | bytes 262176 | tf_op jit(solution)/shard_map/ppermute | solution.py:20
  68.8 2.8 %collective-permute-done.9.refs_2_ = f32[32,2048]{1,0:T(8,128)S(1)} collective-permute-done((f32[32,2048]{1,0:T(8,128)S(1)}, f32[32,2048]{1,0:T(8,128)S(1)}, u32[]{:S(2)}, u32[]{:S(2)}) %collective-permute-start.9) | collective-permute-done | bytes 262176 | tf_op jit(solution)/shard_map/ppermute | solution.py:20
  71.6 5.8 %shard_map.55 = (f32[2,8,32,768]{3,2,1,0:T(8,128)S(1)}, f32[8,128]{1,0:T(8,128)}) custom-call(s32[2]{0:T(128)S(1)} %pad_add_fusion.place, f32[32,4096]{1,0:T(8,128)S(1)} %get-tuple-element.41.refs_0_, f32[32,4096]{1,0:T(8,128)S(1)} %get-tuple-element.42.refs_1_, f32[32,2048]{1,0:T(8,128)S(1)} %collective-permute-done.9.refs_2_, ...), custom_call_target="tpu_custom_call", output_to_operand_aliasing={{0}: (13, {})} | custom-call | flops 8455716864 | bytes 1048576 | tf_op jit(solution)/shard_map/pallas_call | solution.py:97
  77.4 0.1 collective-permute-start.18
  77.5 1.8 %collective-permute-start.20 = (f32[32,2048]{1,0:T(8,128)S(1)}, f32[32,2048]{1,0:T(8,128)S(1)}, u32[]{:S(2)}, u32[]{:S(2)}) collective-permute-start(f32[32,2048]{1,0:T(8,128)S(1)} %collective-permute-done.10.refs_3_), channel_id=1, source_target_pairs={{0,16},{16,0},{32,48},{48,32},{64,80},{80,64},{96,112},{112,96},{1... | collective-permute-start | bytes 786440 | tf_op jit(solution)/shard_map/ppermute | solution.py:25
  79.3 1.9 %collective-permute-start.19 = (f32[32,2048]{1,0:T(8,128)S(1)}, f32[32,2048]{1,0:T(8,128)S(1)}, u32[]{:S(2)}, u32[]{:S(2)}) collective-permute-start(f32[32,2048]{1,0:T(8,128)S(1)} %collective-permute-done.9.refs_2_), channel_id=1, source_target_pairs={{0,16},{16,0},{32,48},{48,32},{64,80},{80,64},{96,112},{112,96},{1... | collective-permute-start | bytes 786440 | tf_op jit(solution)/shard_map/ppermute | solution.py:25
  81.2 7.1 %collective-permute-done.20.refs_0_ = f32[32,2048]{1,0:T(8,128)S(1)} collective-permute-done((f32[32,2048]{1,0:T(8,128)S(1)}, f32[32,2048]{1,0:T(8,128)S(1)}, u32[]{:S(2)}, u32[]{:S(2)}) %collective-permute-start.20) | collective-permute-done | bytes 262176 | tf_op jit(solution)/shard_map/ppermute | solution.py:25
  88.3 2.8 %copy-done.1 = bf16[768,4096]{1,0:T(8,128)(2,1)S(1)} copy-done((bf16[768,4096]{1,0:T(8,128)(2,1)S(1)}, bf16[768,4096]{1,0:T(8,128)(2,1)}, u32[]{:S(2)}) %copy-start.1) | copy-done | bytes 6291480
  91.0 2.8 %copy-done.3 = bf16[768,4096]{1,0:T(8,128)(2,1)S(1)} copy-done((bf16[768,4096]{1,0:T(8,128)(2,1)S(1)}, bf16[768,4096]{1,0:T(8,128)(2,1)}, u32[]{:S(2)}) %copy-start.3) | copy-done | bytes 6291480
  93.8 3.0 %shard_map.56 = (f32[1,1,32,768]{3,2,1,0:T(8,128)S(1)}, f32[8,128]{1,0:T(8,128)}) custom-call(s32[2]{0:T(128)S(1)} %broadcast_1_place.2.place, f32[32,2048]{1,0:T(8,128)S(1)} %collective-permute-done.20.refs_0_, bf16[768,4096]{1,0:T(8,128)(2,1)S(1)} %copy-done.1, bf16[768,4096]{1,0:T(8,128)(2,1)S(1)} %copy-done.3), custom_call_target="tpu_custom_call" | custom-call | flops 603979776 | bytes 1048576 | tf_op jit(solution)/shard_map/pallas_call | solution.py:97
  96.8 3.0 %shard_map.57 = (f32[1,1,32,768]{3,2,1,0:T(8,128)S(1)}, f32[8,128]{1,0:T(8,128)}) custom-call(s32[2]{0:T(128)S(1)} %broadcast_1_place.2.place, f32[32,2048]{1,0:T(8,128)S(1)} %collective-permute-done.19.refs_0_, bf16[768,4096]{1,0:T(8,128)(2,1)S(1)} %copy-done.1, bf16[768,4096]{1,0:T(8,128)(2,1)S(1)} %copy-done.3, ...), custom_call_target="tpu_custom_call", output_to_operand_aliasing={{0}: (4, {})} | custom-call | flops 603979776 | bytes 1048576 | tf_op jit(solution)/shard_map/pallas_call | solution.py:97
  99.8 1.3 %collective-permute-done.21 = f32[32,768]{1,0:T(8,128)S(1)} collective-permute-done((f32[32,768]{1,0:T(8,128)S(1)}, f32[32,768]{1,0:T(8,128)S(1)}, u32[]{:S(2)}, u32[]{:S(2)}) %collective-permute-start.21) | collective-permute-done | bytes 98336 | tf_op jit(solution)/shard_map/ppermute | solution.py:34
  101.1 1.3 %fusion = f32[8,32,768]{2,1,0:T(8,128)S(1)} fusion(f32[8,32,768]{2,1,0:T(8,128)} %collective-permute-done.18, f32[2,8,32,768]{3,2,1,0:T(8,128)S(1)} %get-tuple-element.56, f32[32,768]{1,0:T(8,128)S(1)} %add_select_fusion, pred[8]{0:T(512)(128)(4,1)S(1)} %iota_compare_fusion), kind=kLoop, calls=%fused_computation.1 | loop fusion | flops 589824 | bytes 2457608 | tf_op jit(solution)/shard_map/add | solution.py:258
  102.4 4.8 %collective-permute-start.22 = (f32[32,768]{1,0:T(8,128)S(1)}, f32[32,768]{1,0:T(8,128)S(1)}, u32[]{:S(2)}, u32[]{:S(2)}) collective-permute-start(f32[32,768]{1,0:T(8,128)S(1)} %get-tuple-element.59), channel_id=1, source_target_pairs={{0,10},{2,8},{4,14},{6,12},{8,2},{10,0},{12,6},{14,4},{1,11},{3,9}... | collective-permute-start | bytes 294920 | tf_op jit(solution)/shard_map/ppermute | solution.py:30
  107.2 1.1 collective-permute-start.27
  108.3 1.0 collective-permute-start.26
  109.2 3.7 %collective-permute-start.25 = (f32[32,768]{1,0:T(8,128)S(1)}, f32[32,768]{1,0:T(8,128)S(1)}, u32[]{:S(2)}, u32[]{:S(2)}) collective-permute-start(f32[32,768]{1,0:T(8,128)S(1)} %get-tuple-element.63), channel_id=1, source_target_pairs={{0,14},{2,12},{4,2},{6,0},{8,6},{10,4},{12,10},{14,8},{1,15},{3,13... | collective-permute-start | bytes 294920 | tf_op jit(solution)/shard_map/ppermute | solution.py:30
  113.0 0.7 collective-permute-start.24
  113.6 2.9 %collective-permute-start.23 = (f32[32,768]{1,0:T(8,128)S(1)}, f32[32,768]{1,0:T(8,128)S(1)}, u32[]{:S(2)}, u32[]{:S(2)}) collective-permute-start(f32[32,768]{1,0:T(8,128)S(1)} %get-tuple-element.65), channel_id=1, source_target_pairs={{0,8},{2,10},{4,12},{6,14},{8,0},{10,2},{12,4},{14,6},{1,9},{3,11}... | collective-permute-start | bytes 294920 | tf_op jit(solution)/shard_map/ppermute | solution.py:30
  116.5 4.1 %collective-permute-done.24 = f32[32,768]{1,0:T(8,128)S(1)} collective-permute-done((f32[32,768]{1,0:T(8,128)S(1)}, f32[32,768]{1,0:T(8,128)S(1)}, u32[]{:S(2)}, u32[]{:S(2)}) %collective-permute-start.24) | collective-permute-done | bytes 98336 | tf_op jit(solution)/shard_map/ppermute | solution.py:30
  120.8 0.7 fusion.7
  (44 shorter events, 0.7 us)
Async XLA Ops:
  0.0 18.0 %collective-permute-start.1 = (f32[32,4096]{1,0:T(8,128)}, f32[32,4096]{1,0:T(8,128)S(1)}, u32[]{:S(2)}, u32[]{:S(2)}) collective-permute-start(f32[32,4096]{1,0:T(8,128)} %a0.1), channel_id=1, source_target_pairs={{0,32},{16,48},{32,64},{48,80},{64,96},{80,112},{96,128},{112,144}... | collective-permute-start | bytes 1572872 | tf_op jit(solution)/shard_map/ppermute | solution.py:20
  1.9 16.1 %collective-permute-start = (f32[32,4096]{1,0:T(8,128)}, f32[32,4096]{1,0:T(8,128)S(1)}, u32[]{:S(2)}, u32[]{:S(2)}) collective-permute-start(f32[32,4096]{1,0:T(8,128)} %a0.1), channel_id=1, source_target_pairs={{0,224},{16,240},{32,0},{48,16},{64,32},{80,48},{96,64},{112,80},{... | collective-permute-start | bytes 1572872 | tf_op jit(solution)/shard_map/ppermute | solution.py:20
  5.9 15.1 %collective-permute-start.2 = (f32[32,4096]{1,0:T(8,128)}, f32[32,4096]{1,0:T(8,128)S(1)}, u32[]{:S(2)}, u32[]{:S(2)}) collective-permute-start(f32[32,4096]{1,0:T(8,128)} %a0.1), channel_id=1, source_target_pairs={{0,16},{16,0},{32,48},{48,32},{64,80},{80,64},{96,112},{112,96},{1... | collective-permute-start | bytes 1572872 | tf_op jit(solution)/shard_map/ppermute | solution.py:25
  8.1 1.0 copy-start.4
  16.6 55.0 %copy-start = (bf16[768,4096]{1,0:T(8,128)(2,1)}, bf16[768,4096]{1,0:T(8,128)(2,1)S(1)}, u32[]{:S(2)}) copy-start(bf16[768,4096]{1,0:T(8,128)(2,1)S(1)} %get-tuple-element.32.refs_3_.refs_2_.refs_1_.refs_5_.refs_10_) | copy-start | bytes 18874372
  16.6 55.0 %copy-start.2 = (bf16[768,4096]{1,0:T(8,128)(2,1)}, bf16[768,4096]{1,0:T(8,128)(2,1)S(1)}, u32[]{:S(2)}) copy-start(bf16[768,4096]{1,0:T(8,128)(2,1)S(1)} %get-tuple-element.33.refs_4_.refs_3_.refs_2_.refs_6_.refs_11_) | copy-start | bytes 18874372
  21.0 14.1 %collective-permute-start.5 = (f32[32,4096]{1,0:T(8,128)S(1)}, f32[32,4096]{1,0:T(8,128)S(1)}, u32[]{:S(2)}, u32[]{:S(2)}) collective-permute-start(f32[32,4096]{1,0:T(8,128)S(1)} %get-tuple-element.37), channel_id=1, source_target_pairs={{0,16},{16,0},{32,48},{48,32},{64,80},{80,64},{96,112},{112,96},{1... | collective-permute-start | bytes 1572872 | tf_op jit(solution)/shard_map/ppermute | solution.py:25
  23.2 14.9 %collective-permute-start.3 = (f32[32,4096]{1,0:T(8,128)S(1)}, f32[32,4096]{1,0:T(8,128)S(1)}, u32[]{:S(2)}, u32[]{:S(2)}) collective-permute-start(f32[32,4096]{1,0:T(8,128)S(1)} %get-tuple-element.35.refs_1_), channel_id=1, source_target_pairs={{0,224},{16,240},{32,0},{48,16},{64,32},{80,48},{96,64},{112,80},{... | collective-permute-start | bytes 1572872 | tf_op jit(solution)/shard_map/ppermute | solution.py:20
  25.0 16.1 %collective-permute-start.4 = (f32[32,4096]{1,0:T(8,128)S(1)}, f32[32,4096]{1,0:T(8,128)S(1)}, u32[]{:S(2)}, u32[]{:S(2)}) collective-permute-start(f32[32,4096]{1,0:T(8,128)S(1)} %get-tuple-element.36.refs_0_), channel_id=1, source_target_pairs={{0,32},{16,48},{32,64},{48,80},{64,96},{80,112},{96,128},{112,144}... | collective-permute-start | bytes 1572872 | tf_op jit(solution)/shard_map/ppermute | solution.py:20
  29.9 16.8 %collective-permute-start.12 = (f32[16,4096]{1,0:T(8,128)S(1)}, f32[16,4096]{1,0:T(8,128)S(1)}, u32[]{:S(2)}, u32[]{:S(2)}) collective-permute-start(f32[16,4096]{1,0:T(8,128)S(1)} %shard_map.51), channel_id=1, source_target_pairs={{0,32},{16,48},{32,64},{48,80},{64,96},{80,112},{96,128},{112,144}... | collective-permute-start | bytes 786440 | tf_op jit(solution)/shard_map/ppermute | solution.py:20
  30.0 16.7 %collective-permute-start.11 = (f32[16,4096]{1,0:T(8,128)S(1)}, f32[16,4096]{1,0:T(8,128)S(1)}, u32[]{:S(2)}, u32[]{:S(2)}) collective-permute-start(f32[16,4096]{1,0:T(8,128)S(1)} %shard_map.51), channel_id=1, source_target_pairs={{0,224},{16,240},{32,0},{48,16},{64,32},{80,48},{96,64},{112,80},{... | collective-permute-start | bytes 786440 | tf_op jit(solution)/shard_map/ppermute | solution.py:20
  41.1 12.0 %collective-permute-start.8 = (f32[32,4096]{1,0:T(8,128)S(1)}, f32[32,4096]{1,0:T(8,128)S(1)}, u32[]{:S(2)}, u32[]{:S(2)}) collective-permute-start(f32[32,4096]{1,0:T(8,128)S(1)} %get-tuple-element.40), channel_id=1, source_target_pairs={{0,16},{16,0},{32,48},{48,32},{64,80},{80,64},{96,112},{112,96},{1... | collective-permute-start | bytes 1572872 | tf_op jit(solution)/shard_map/ppermute | solution.py:25
  42.1 12.9 %collective-permute-start.6 = (f32[32,4096]{1,0:T(8,128)S(1)}, f32[32,4096]{1,0:T(8,128)S(1)}, u32[]{:S(2)}, u32[]{:S(2)}) collective-permute-start(f32[32,4096]{1,0:T(8,128)S(1)} %get-tuple-element.38.refs_3_), channel_id=1, source_target_pairs={{0,224},{16,240},{32,0},{48,16},{64,32},{80,48},{96,64},{112,80},{... | collective-permute-start | bytes 1572872 | tf_op jit(solution)/shard_map/ppermute | solution.py:20
  42.4 15.0 %collective-permute-start.7 = (f32[32,4096]{1,0:T(8,128)S(1)}, f32[32,4096]{1,0:T(8,128)S(1)}, u32[]{:S(2)}, u32[]{:S(2)}) collective-permute-start(f32[32,4096]{1,0:T(8,128)S(1)} %get-tuple-element.39.refs_2_), channel_id=1, source_target_pairs={{0,32},{16,48},{32,64},{48,80},{64,96},{80,112},{96,128},{112,144}... | collective-permute-start | bytes 1572872 | tf_op jit(solution)/shard_map/ppermute | solution.py:20
  51.0 8.1 %collective-permute-start.13 = (f32[16,4096]{1,0:T(8,128)S(1)}, f32[16,4096]{1,0:T(8,128)S(1)}, u32[]{:S(2)}, u32[]{:S(2)}) collective-permute-start(f32[16,4096]{1,0:T(8,128)S(1)} %get-tuple-element.50), channel_id=1, source_target_pairs={{0,224},{16,240},{32,0},{48,16},{64,32},{80,48},{96,64},{112,80},{... | collective-permute-start | bytes 786440 | tf_op jit(solution)/shard_map/ppermute | solution.py:20
  51.0 9.2 %collective-permute-start.14 = (f32[16,4096]{1,0:T(8,128)S(1)}, f32[16,4096]{1,0:T(8,128)S(1)}, u32[]{:S(2)}, u32[]{:S(2)}) collective-permute-start(f32[16,4096]{1,0:T(8,128)S(1)} %get-tuple-element.51), channel_id=1, source_target_pairs={{0,32},{16,48},{32,64},{48,80},{64,96},{80,112},{96,128},{112,144}... | collective-permute-start | bytes 786440 | tf_op jit(solution)/shard_map/ppermute | solution.py:20
  57.5 14.0 %collective-permute-start.17 = (f32[32,4096]{1,0:T(8,128)S(1)}, f32[32,4096]{1,0:T(8,128)S(1)}, u32[]{:S(2)}, u32[]{:S(2)}) collective-permute-start(f32[32,4096]{1,0:T(8,128)S(1)} %get-tuple-element.52.refs_4_), channel_id=1, source_target_pairs={{0,16},{16,0},{32,48},{48,32},{64,80},{80,64},{96,112},{112,96},{1... | collective-permute-start | bytes 1572872 | tf_op jit(solution)/shard_map/ppermute | solution.py:25
  60.3 8.5 %collective-permute-start.15 = (f32[16,4096]{1,0:T(8,128)S(1)}, f32[16,4096]{1,0:T(8,128)S(1)}, u32[]{:S(2)}, u32[]{:S(2)}) collective-permute-start(f32[16,4096]{1,0:T(8,128)S(1)} %get-tuple-element.53.refs_4_), channel_id=1, source_target_pairs={{0,32},{16,48},{32,64},{48,80},{64,96},{80,112},{96,128},{112,144}... | collective-permute-start | bytes 786440 | tf_op jit(solution)/shard_map/ppermute | solution.py:20
  60.3 8.5 %collective-permute-start.16 = (f32[16,4096]{1,0:T(8,128)S(1)}, f32[16,4096]{1,0:T(8,128)S(1)}, u32[]{:S(2)}, u32[]{:S(2)}) collective-permute-start(f32[16,4096]{1,0:T(8,128)S(1)} %get-tuple-element.54.refs_5_), channel_id=1, source_target_pairs={{0,224},{16,240},{32,0},{48,16},{64,32},{80,48},{96,64},{112,80},{... | collective-permute-start | bytes 786440 | tf_op jit(solution)/shard_map/ppermute | solution.py:20
  63.5 8.1 %collective-permute-start.9 = (f32[32,2048]{1,0:T(8,128)S(1)}, f32[32,2048]{1,0:T(8,128)S(1)}, u32[]{:S(2)}, u32[]{:S(2)}) collective-permute-start(f32[32,2048]{1,0:T(8,128)S(1)} %get-tuple-element.43), channel_id=1, source_target_pairs={{0,32},{16,48},{32,64},{48,80},{64,96},{80,112},{96,128},{112,144}... | collective-permute-start | bytes 786440 | tf_op jit(solution)/shard_map/ppermute | solution.py:20
  63.5 8.1 %collective-permute-start.10 = (f32[32,2048]{1,0:T(8,128)S(1)}, f32[32,2048]{1,0:T(8,128)S(1)}, u32[]{:S(2)}, u32[]{:S(2)}) collective-permute-start(f32[32,2048]{1,0:T(8,128)S(1)} %get-tuple-element.44), channel_id=1, source_target_pairs={{0,224},{16,240},{32,0},{48,16},{64,32},{80,48},{96,64},{112,80},{... | collective-permute-start | bytes 786440 | tf_op jit(solution)/shard_map/ppermute | solution.py:20
  77.4 23.6 %collective-permute-start.18 = (f32[8,32,768]{2,1,0:T(8,128)S(1)}, f32[8,32,768]{2,1,0:T(8,128)}, u32[]{:S(2)}, u32[]{:S(2)}) collective-permute-start(f32[8,32,768]{2,1,0:T(8,128)S(1)} %slice_bitcast_fusion), channel_id=1, source_target_pairs={{0,1},{1,0},{2,3},{3,2},{4,5},{5,4},{6,7},{7,6},{8,9},{9,8},{10,11... | collective-permute-start | bytes 2359304 | tf_op jit(solution)/shard_map/ppermute | solution.py:34
  77.5 10.7 %collective-permute-start.20 = (f32[32,2048]{1,0:T(8,128)S(1)}, f32[32,2048]{1,0:T(8,128)S(1)}, u32[]{:S(2)}, u32[]{:S(2)}) collective-permute-start(f32[32,2048]{1,0:T(8,128)S(1)} %collective-permute-done.10.refs_3_), channel_id=1, source_target_pairs={{0,16},{16,0},{32,48},{48,32},{64,80},{80,64},{96,112},{112,96},{1... | collective-permute-start | bytes 786440 | tf_op jit(solution)/shard_map/ppermute | solution.py:25
  79.3 17.5 %collective-permute-start.19 = (f32[32,2048]{1,0:T(8,128)S(1)}, f32[32,2048]{1,0:T(8,128)S(1)}, u32[]{:S(2)}, u32[]{:S(2)}) collective-permute-start(f32[32,2048]{1,0:T(8,128)S(1)} %collective-permute-done.9.refs_2_), channel_id=1, source_target_pairs={{0,16},{16,0},{32,48},{48,32},{64,80},{80,64},{96,112},{112,96},{1... | collective-permute-start | bytes 786440 | tf_op jit(solution)/shard_map/ppermute | solution.py:25
  88.3 2.8 %copy-start.1 = (bf16[768,4096]{1,0:T(8,128)(2,1)S(1)}, bf16[768,4096]{1,0:T(8,128)(2,1)}, u32[]{:S(2)}) copy-start(bf16[768,4096]{1,0:T(8,128)(2,1)} %copy-done) | copy-start | bytes 18874372
  91.0 2.8 %copy-start.3 = (bf16[768,4096]{1,0:T(8,128)(2,1)S(1)}, bf16[768,4096]{1,0:T(8,128)(2,1)}, u32[]{:S(2)}) copy-start(bf16[768,4096]{1,0:T(8,128)(2,1)} %copy-done.2) | copy-start | bytes 18874372
  99.7 1.3 %collective-permute-start.21 = (f32[32,768]{1,0:T(8,128)S(1)}, f32[32,768]{1,0:T(8,128)S(1)}, u32[]{:S(2)}, u32[]{:S(2)}) collective-permute-start(f32[32,768]{1,0:T(8,128)S(1)} %bitcast.41), channel_id=1, source_target_pairs={{0,1},{1,0},{2,3},{3,2},{4,5},{5,4},{6,7},{7,6},{8,9},{9,8},{10,11... | collective-permute-start | bytes 294920 | tf_op jit(solution)/shard_map/ppermute | solution.py:34
  101.1 19.7 %copy-start.5 = (f32[768]{0:T(1024)S(1)}, f32[768]{0:T(1024)}, u32[]{:S(2)}) copy-start(f32[768]{0:T(1024)} %param.7) | copy-start | bytes 9220
  101.1 19.7 %copy-start.6 = (f32[32]{0:T(128)S(1)}, f32[32]{0:T(128)}, u32[]{:S(2)}) copy-start(f32[32]{0:T(128)} %param.6) | copy-start | bytes 388
  102.4 10.5 %collective-permute-start.22 = (f32[32,768]{1,0:T(8,128)S(1)}, f32[32,768]{1,0:T(8,128)S(1)}, u32[]{:S(2)}, u32[]{:S(2)}) collective-permute-start(f32[32,768]{1,0:T(8,128)S(1)} %get-tuple-element.59), channel_id=1, source_target_pairs={{0,10},{2,8},{4,14},{6,12},{8,2},{10,0},{12,6},{14,4},{1,11},{3,9}... | collective-permute-start | bytes 294920 | tf_op jit(solution)/shard_map/ppermute | solution.py:30
  107.2 6.4 %collective-permute-start.28 = (f32[32,768]{1,0:T(8,128)S(1)}, f32[32,768]{1,0:T(8,128)S(1)}, u32[]{:S(2)}, u32[]{:S(2)}) collective-permute-start(f32[32,768]{1,0:T(8,128)S(1)} %get-tuple-element.60), channel_id=1, source_target_pairs={{0,2},{2,0},{4,6},{6,4},{8,10},{10,8},{12,14},{14,12},{1,3},{3,1},... | collective-permute-start | bytes 294920 | tf_op jit(solution)/shard_map/ppermute | solution.py:30
  107.2 9.3 %collective-permute-start.27 = (f32[32,768]{1,0:T(8,128)S(1)}, f32[32,768]{1,0:T(8,128)S(1)}, u32[]{:S(2)}, u32[]{:S(2)}) collective-permute-start(f32[32,768]{1,0:T(8,128)S(1)} %get-tuple-element.61), channel_id=1, source_target_pairs={{0,12},{2,14},{4,0},{6,2},{8,4},{10,6},{12,8},{14,10},{1,13},{3,15... | collective-permute-start | bytes 294920 | tf_op jit(solution)/shard_map/ppermute | solution.py:30
  108.3 8.3 %collective-permute-start.26 = (f32[32,768]{1,0:T(8,128)S(1)}, f32[32,768]{1,0:T(8,128)S(1)}, u32[]{:S(2)}, u32[]{:S(2)}) collective-permute-start(f32[32,768]{1,0:T(8,128)S(1)} %get-tuple-element.62), channel_id=1, source_target_pairs={{0,4},{2,6},{4,8},{6,10},{8,12},{10,14},{12,0},{14,2},{1,5},{3,7},... | collective-permute-start | bytes 294920 | tf_op jit(solution)/shard_map/ppermute | solution.py:30
  109.2 7.3 %collective-permute-start.25 = (f32[32,768]{1,0:T(8,128)S(1)}, f32[32,768]{1,0:T(8,128)S(1)}, u32[]{:S(2)}, u32[]{:S(2)}) collective-permute-start(f32[32,768]{1,0:T(8,128)S(1)} %get-tuple-element.63), channel_id=1, source_target_pairs={{0,14},{2,12},{4,2},{6,0},{8,6},{10,4},{12,10},{14,8},{1,15},{3,13... | collective-permute-start | bytes 294920 | tf_op jit(solution)/shard_map/ppermute | solution.py:30
  113.0 7.7 %collective-permute-start.24 = (f32[32,768]{1,0:T(8,128)S(1)}, f32[32,768]{1,0:T(8,128)S(1)}, u32[]{:S(2)}, u32[]{:S(2)}) collective-permute-start(f32[32,768]{1,0:T(8,128)S(1)} %get-tuple-element.64), channel_id=1, source_target_pairs={{0,6},{2,4},{4,10},{6,8},{8,14},{10,12},{12,2},{14,0},{1,7},{3,5},... | collective-permute-start | bytes 294920 | tf_op jit(solution)/shard_map/ppermute | solution.py:30
  113.6 7.1 %collective-permute-start.23 = (f32[32,768]{1,0:T(8,128)S(1)}, f32[32,768]{1,0:T(8,128)S(1)}, u32[]{:S(2)}, u32[]{:S(2)}) collective-permute-start(f32[32,768]{1,0:T(8,128)S(1)} %get-tuple-element.65), channel_id=1, source_target_pairs={{0,8},{2,10},{4,12},{6,14},{8,0},{10,2},{12,4},{14,6},{1,9},{3,11}... | collective-permute-start | bytes 294920 | tf_op jit(solution)/shard_map/ppermute | solution.py:30
